TPU v7x, 512 devices: a whole 4x8x8 slice. The times are simulated.
512 devices in a mesh: seq: 32 (over z_lo, y), pipe: 4 (over x), dp: 4 (over z_hi, core).
Axes of the slice: x: 4, y: 8, z: 8 (z_hi: 2, z_lo: 4; z = z_hi * 4 + z_lo), core: 2. Of those that a mesh axis runs over, the one named last changes fastest.
Arguments:
- section_inputs: bfloat16 [4, 4, 32, 256, 12, 128], P('pipe', 'dp', 'seq'), may hold values from -6 to 6
- out_grad: bfloat16 [4, 32, 256, 12, 128], P('dp', 'seq'), may hold values from -6 to 6
- gains: float32 [4, 2, 2, 12, 128], P('pipe'), may hold values from -16 to 16
Outputs:
- input_grads: bfloat16 [4, 4, 32, 256, 12, 128], P('pipe', 'dp', 'seq')
- gain_grads: float32 [4, 2, 2, 12, 128], P('pipe')
All inputs are finite; a program needn't handle non-finite values.
Results may differ from a plain program's by a relative error of at most 0.035.
Values may be sent and summed in bfloat16 or wider, within the bound.
A program may use at most 64 MiB of HBM per device.

v0:
```python
from functools import partial

import jax
import jax.numpy as jnp
from jax import lax
from jax.sharding import PartitionSpec as P


def passed_along(block, axis, distance):
    devices = range(lax.axis_size(axis))
    route = [(i - distance, i) for i in devices if i - distance in devices]
    return lax.ppermute(block, axis, route)


def normed(values):
    return values * lax.rsqrt(jnp.mean(values * values, axis=-1, keepdims=True) + 1e-06)


def attend(values, gain_q, gain_k, score_form, mix_form):
    rows = normed(values)
    query = (rows * gain_q).astype(jnp.bfloat16)
    keys_part = (rows * gain_k).astype(jnp.bfloat16)
    scores = jnp.einsum(
        score_form, query, keys_part, preferred_element_type=jnp.float32
    ) * values.shape[-1] ** (-0.5)
    weights = jax.nn.softmax(scores, axis=-1).astype(jnp.bfloat16)
    return jnp.einsum(
        mix_form, weights, values.astype(jnp.bfloat16), preferred_element_type=jnp.float32
    )


def spatial_core(values, gain_q, gain_k):
    return attend(values, gain_q, gain_k, "bfshd,bfthd->bfhst", "bfhst,bfthd->bfshd")


def temporal_core(values, gain_q, gain_k):
    return attend(values, gain_q, gain_k, "bfshd,bgshd->bshfg", "bshfg,bgshd->bfshd")


def apply_back(back_fn, cotangent):
    return back_fn(cotangent)


def per_device(section_inputs, out_grad, gains):
    inputs_local = section_inputs[0]
    gain_local = gains[0]
    pipe_count = lax.axis_size("pipe")
    section_index = lax.axis_index("pipe")
    micro_count = inputs_local.shape[0]
    steps_total = micro_count + pipe_count - 1
    block_shape = (1,) + inputs_local.shape[1:]
    single = inputs_local.astype(jnp.float32)
    primal, back_one = jax.vjp(spatial_core, single, gain_local[0, 0], gain_local[0, 1])
    mixed_parts = (single + primal).astype(jnp.bfloat16)
    back_list = [partial(apply_back, back_one)]
    mixed_all = lax.all_to_all(mixed_parts, "seq", split_axis=2, concat_axis=1, tiled=True)
    grads_local = jnp.zeros(inputs_local.shape, jnp.bfloat16)
    gain_total = jnp.zeros(gain_local.shape, jnp.float32)
    carried = jnp.zeros(block_shape, jnp.bfloat16)
    for phase_step in range(steps_total):
        micro = phase_step - (pipe_count - 1 - section_index)
        usable = jnp.logical_and(micro >= 0, micro < micro_count)
        micro_index = jnp.clip(micro, 0, micro_count - 1)
        grad_block = jnp.where(section_index == pipe_count - 1, out_grad, carried)
        grad_time = lax.all_to_all(grad_block, "seq", split_axis=2, concat_axis=1, tiled=True)
        undo_space = partial(lax.switch, micro_index, back_list)
        mixed_float = lax.optimization_barrier(mixed_all).astype(jnp.float32)
        _, back_time = jax.vjp(temporal_core, mixed_float, gain_local[1, 0], gain_local[1, 1])
        time_grad, time_gq, time_gk = back_time(grad_time.astype(jnp.float32))
        resid_time = (grad_time.astype(jnp.float32) + time_grad).astype(jnp.bfloat16)
        resid_space = lax.all_to_all(resid_time, "seq", split_axis=1, concat_axis=2, tiled=True)
        space_grad, space_gq, space_gk = undo_space(resid_space.astype(jnp.float32))
        input_grad = (resid_space.astype(jnp.float32) + space_grad).astype(jnp.bfloat16)
        updated = lax.dynamic_update_slice_in_dim(grads_local, input_grad, micro_index, 0)
        grads_local = jnp.where(usable, updated, grads_local)
        step_gains = jnp.stack([jnp.stack([space_gq, space_gk]), jnp.stack([time_gq, time_gk])])
        step_gains = jnp.where(usable, step_gains, jnp.zeros_like(step_gains))
        gain_total = gain_total + step_gains
        if phase_step + 1 < steps_total:
            carried = passed_along(input_grad, "pipe", -1)
    gain_total = lax.psum(gain_total, ("seq", "dp"))
    return (grads_local[None], gain_total[None])


def solution(mesh):
    return jax.shard_map(
        per_device,
        mesh=mesh,
        in_specs=(
            P("pipe", "dp", "seq", None, None, None),
            P("dp", "seq", None, None, None),
            P("pipe", None, None, None, None),
        ),
        out_specs=(P("pipe", "dp", "seq", None, None, None), P("pipe", None, None, None, None)),
        check_vma=False,
    )
```

profile of v0, /device:TPU:36, one launch (start us, length us, event | category | flops | bytes accessed | tf_op | source)
XLA Modules:
  0.0 1087.1 jit_solution(610661340901445155)
XLA Ops:
  3.1 3.4 fusion.265
  10.3 12.8 %all-to-all-start.1 = ((bf16[1,1,256,12,128]{4,3,1,0,2:T(8,128)(2,1)}), bf16[1,1,256,12,128]{4,3,1,0,2:T(8,128)(2,1)}, u32[]{:S(2)}, u32[]{:S(2)}) async-start(bf16[1,1,256,12,128]{4,3,1,0,2:T(8,128)(2,1)} %copy.143), calls=%async_computation.1 | async-start | bytes 2097152 | tf_op jit(solution)/shard_map/all_to_all | solution.py:56
  24.7 23.3 %all-to-all-done.1 = bf16[1,1,256,12,128]{4,3,1,0,2:T(8,128)(2,1)} async-done(((bf16[1,1,256,12,128]{4,3,1,0,2:T(8,128)(2,1)}), bf16[1,1,256,12,128]{4,3,1,0,2:T(8,128)(2,1)}, u32[]{:S(2)}, u32[]{:S(2)}) %all-to-all-start.1) | async-done | bytes 786464 | tf_op jit(solution)/shard_map/all_to_all | solution.py:56
  48.0 8.9 all-to-all-start
  59.8 3.6 fusion.266
  63.4 18.6 %all-to-all-done = bf16[1,1,256,12,128]{4,3,1,0,2:T(8,128)(2,1)} async-done(((bf16[1,1,256,12,128]{4,3,1,0,2:T(8,128)(2,1)}), bf16[1,1,256,12,128]{4,3,1,0,2:T(8,128)(2,1)}, u32[]{:S(2)}, u32[]{:S(2)}) %all-to-all-start) | async-done | bytes 786464 | tf_op jit(solution)/shard_map/all_to_all | solution.py:65
  91.7 8.6 all-to-all-start.2
  100.3 19.3 %all-to-all-done.2 = bf16[1,32,8,12,128]{4,2,3,0,1:T(8,128)(2,1)} async-done(((bf16[1,32,8,12,128]{4,2,3,0,1:T(8,128)(2,1)}), bf16[1,32,8,12,128]{4,2,3,0,1:T(8,128)(2,1)}, u32[]{:S(2)}, u32[]{:S(2)}) %all-to-all-start.2) | async-done | bytes 786464 | tf_op jit(solution)/shard_map/all_to_all | solution.py:71
  130.4 17.2 %collective-permute-done = bf16[1,1,256,12,128]{4,2,3,1,0:T(8,128)(2,1)S(1)} collective-permute-done((bf16[1,1,256,12,128]{4,2,3,1,0:T(8,128)(2,1)S(1)}, bf16[1,1,256,12,128]{4,2,3,1,0:T(8,128)(2,1)S(1)}, u32[]{:S(2)}, u32[]{:S(2)}) %collective-permute-start) | collective-permute-done | bytes 786464 | tf_op jit(solution)/shard_map/ppermute | solution.py:12
  148.2 34.6 %all_to_all.108 = bf16[1,1,256,12,128]{4,3,1,0,2:T(8,128)(2,1)S(1)} all-to-all(bf16[1,1,256,12,128]{4,3,1,0,2:T(8,128)(2,1)S(1)} %copy.155), channel_id=1, replica_groups=mesh['seq'=32,'pipe'=4,'dp'=4] {'seq'}, dimensions={2} | all-to-all | bytes 1572864 | tf_op jit(solution)/shard_map/all_to_all | solution.py:65
  188.7 27.3 %all_to_all.109 = bf16[1,32,8,12,128]{4,2,3,0,1:T(8,128)(2,1)S(1)} all-to-all(bf16[1,32,8,12,128]{4,2,3,0,1:T(8,128)(2,1)S(1)} %copy.161), channel_id=1, replica_groups=mesh['seq'=32,'pipe'=4,'dp'=4] {'seq'}, dimensions={1} | all-to-all | bytes 1572864 | tf_op jit(solution)/shard_map/all_to_all | solution.py:71
  217.9 3.0 fusion.82
  224.6 17.3 %collective-permute-done.1 = bf16[1,1,256,12,128]{4,2,3,1,0:T(8,128)(2,1)S(1)} collective-permute-done((bf16[1,1,256,12,128]{4,2,3,1,0:T(8,128)(2,1)S(1)}, bf16[1,1,256,12,128]{4,2,3,1,0:T(8,128)(2,1)S(1)}, u32[]{:S(2)}, u32[]{:S(2)}) %collective-permute-start.1) | collective-permute-done | bytes 786464 | tf_op jit(solution)/shard_map/ppermute | solution.py:12
  242.6 34.5 %all_to_all.110 = bf16[1,1,256,12,128]{4,3,1,0,2:T(8,128)(2,1)S(1)} all-to-all(bf16[1,1,256,12,128]{4,3,1,0,2:T(8,128)(2,1)S(1)} %copy.168), channel_id=1, replica_groups=mesh['seq'=32,'pipe'=4,'dp'=4] {'seq'}, dimensions={2} | all-to-all | bytes 1572864 | tf_op jit(solution)/shard_map/all_to_all | solution.py:65
  278.9 2.8 fusion.94
  283.5 27.4 %all_to_all.111 = bf16[1,32,8,12,128]{4,2,3,0,1:T(8,128)(2,1)S(1)} all-to-all(bf16[1,32,8,12,128]{4,2,3,0,1:T(8,128)(2,1)S(1)} %copy.174), channel_id=1, replica_groups=mesh['seq'=32,'pipe'=4,'dp'=4] {'seq'}, dimensions={1} | all-to-all | bytes 1572864 | tf_op jit(solution)/shard_map/all_to_all | solution.py:71
  312.8 3.0 fusion.84
  319.5 17.4 %collective-permute-done.2 = bf16[1,1,256,12,128]{4,2,3,1,0:T(8,128)(2,1)S(1)} collective-permute-done((bf16[1,1,256,12,128]{4,2,3,1,0:T(8,128)(2,1)S(1)}, bf16[1,1,256,12,128]{4,2,3,1,0:T(8,128)(2,1)S(1)}, u32[]{:S(2)}, u32[]{:S(2)}) %collective-permute-start.2) | collective-permute-done | bytes 786464 | tf_op jit(solution)/shard_map/ppermute | solution.py:12
  337.5 34.3 %all_to_all.112 = bf16[1,1,256,12,128]{4,3,1,0,2:T(8,128)(2,1)S(1)} all-to-all(bf16[1,1,256,12,128]{4,3,1,0,2:T(8,128)(2,1)S(1)} %copy.181), channel_id=1, replica_groups=mesh['seq'=32,'pipe'=4,'dp'=4] {'seq'}, dimensions={2} | all-to-all | bytes 1572864 | tf_op jit(solution)/shard_map/all_to_all | solution.py:65
  379.3 8.7 all-to-all-start.8
  388.4 18.3 %all-to-all-done.8 = bf16[1,32,8,12,128]{4,2,3,0,1:T(8,128)(2,1)} async-done(((bf16[1,32,8,12,128]{4,2,3,0,1:T(8,128)(2,1)}), bf16[1,32,8,12,128]{4,2,3,0,1:T(8,128)(2,1)}, u32[]{:S(2)}, u32[]{:S(2)}) %all-to-all-start.8) | async-done | bytes 786464 | tf_op jit(solution)/shard_map/all_to_all | solution.py:71
  410.1 3.0 fusion.86
  413.3 668.9 %psum.7 = f32[1,2,2,12,128]{4,2,3,1,0:T(2,128)} all-reduce(f32[1,2,2,12,128]{4,2,3,1,0:T(2,128)S(1)} %fusion.218), channel_id=1, replica_groups=mesh['seq'=32,'pipe'=4,'dp'=4] {'seq','dp'}, use_global_device_ids=true, to_apply=%region_38.39 | all-reduce | flops 6144 | bytes 49152 | tf_op jit(solution)/shard_map/psum | solution.py:81
  1082.2 5.0 fusion.168
  (151 shorter events, 64.4 us)
Async XLA Ops:
  10.3 37.7 %all-to-all-start.1 = ((bf16[1,1,256,12,128]{4,3,1,0,2:T(8,128)(2,1)}), bf16[1,1,256,12,128]{4,3,1,0,2:T(8,128)(2,1)}, u32[]{:S(2)}, u32[]{:S(2)}) async-start(bf16[1,1,256,12,128]{4,3,1,0,2:T(8,128)(2,1)} %copy.143), calls=%async_computation.1 | async-start | bytes 2097152 | tf_op jit(solution)/shard_map/all_to_all | solution.py:56
  48.0 34.0 %all-to-all-start = ((bf16[1,1,256,12,128]{4,3,1,0,2:T(8,128)(2,1)}), bf16[1,1,256,12,128]{4,3,1,0,2:T(8,128)(2,1)}, u32[]{:S(2)}, u32[]{:S(2)}) async-start(bf16[1,1,256,12,128]{4,3,1,0,2:T(8,128)(2,1)} %copy.138), calls=%async_computation | async-start | bytes 2097152 | tf_op jit(solution)/shard_map/all_to_all | solution.py:65
  85.8 3.2 copy-start.22
  91.7 27.9 %all-to-all-start.2 = ((bf16[1,32,8,12,128]{4,2,3,0,1:T(8,128)(2,1)}), bf16[1,32,8,12,128]{4,2,3,0,1:T(8,128)(2,1)}, u32[]{:S(2)}, u32[]{:S(2)}) async-start(bf16[1,32,8,12,128]{4,2,3,0,1:T(8,128)(2,1)} %copy.148), calls=%async_computation.2 | async-start | bytes 1572864 | tf_op jit(solution)/shard_map/all_to_all | solution.py:71
  123.0 2.5 copy-start.10
  125.4 22.1 %copy-start.8 = (bf16[1,1,256,12,128]{4,2,3,1,0:T(8,128)(2,1)S(1)}, bf16[1,1,256,12,128]{4,2,3,1,0:T(8,128)(2,1)}, u32[]{:S(2)}) copy-start(bf16[1,1,256,12,128]{4,2,3,1,0:T(8,128)(2,1)} %param.4) | copy-start | bytes 2359300
  127.9 2.5 copy-start.19
  127.9 19.6 %collective-permute-start = (bf16[1,1,256,12,128]{4,2,3,1,0:T(8,128)(2,1)S(1)}, bf16[1,1,256,12,128]{4,2,3,1,0:T(8,128)(2,1)S(1)}, u32[]{:S(2)}, u32[]{:S(2)}) collective-permute-start(bf16[1,1,256,12,128]{4,2,3,1,0:T(8,128)(2,1)S(1)} %fusion.67), channel_id=1, source_target_pairs={{4,0},{8,4},{12,8},{5,1},{9,5},{13,9},{6,2},{10,6},{14,10},{7,3},{... | collective-permute-start | bytes 2359304 | tf_op jit(solution)/shard_map/ppermute | solution.py:12
  148.2 34.8 %copy-start.5 = (bf16[1,1,256,12,128]{4,2,3,1,0:T(8,128)(2,1)S(1)}, bf16[1,1,256,12,128]{4,2,3,1,0:T(8,128)(2,1)}, u32[]{:S(2)}) copy-start(bf16[1,1,256,12,128]{4,2,3,1,0:T(8,128)(2,1)} %copy-done.3) | copy-start | bytes 2359300
  148.2 34.8 %copy-start.7 = (f32[8,12,32,32]{2,3,1,0:T(8,128)S(1)}, f32[8,12,32,32]{2,3,1,0:T(8,128)}, u32[]{:S(2)}) copy-start(f32[8,12,32,32]{2,3,1,0:T(8,128)} %get-tuple-element.35) | copy-start | bytes 1179652
  222.1 20.4 %copy-start.20 = (bf16[1,1,256,12,128]{4,2,3,1,0:T(8,128)(2,1)}, bf16[1,1,256,12,128]{4,2,3,1,0:T(8,128)(2,1)S(1)}, u32[]{:S(2)}) copy-start(bf16[1,1,256,12,128]{4,2,3,1,0:T(8,128)(2,1)S(1)} %fusion.71) | copy-start | bytes 2359300
  222.1 19.8 %collective-permute-start.1 = (bf16[1,1,256,12,128]{4,2,3,1,0:T(8,128)(2,1)S(1)}, bf16[1,1,256,12,128]{4,2,3,1,0:T(8,128)(2,1)S(1)}, u32[]{:S(2)}, u32[]{:S(2)}) collective-permute-start(bf16[1,1,256,12,128]{4,2,3,1,0:T(8,128)(2,1)S(1)} %fusion.71), channel_id=1, source_target_pairs={{4,0},{8,4},{12,8},{5,1},{9,5},{13,9},{6,2},{10,6},{14,10},{7,3},{... | collective-permute-start | bytes 2359304 | tf_op jit(solution)/shard_map/ppermute | solution.py:12
  317.0 20.5 %copy-start.21 = (bf16[1,1,256,12,128]{4,2,3,1,0:T(8,128)(2,1)}, bf16[1,1,256,12,128]{4,2,3,1,0:T(8,128)(2,1)S(1)}, u32[]{:S(2)}) copy-start(bf16[1,1,256,12,128]{4,2,3,1,0:T(8,128)(2,1)S(1)} %fusion.75) | copy-start | bytes 2359300
  317.1 19.8 %collective-permute-start.2 = (bf16[1,1,256,12,128]{4,2,3,1,0:T(8,128)(2,1)S(1)}, bf16[1,1,256,12,128]{4,2,3,1,0:T(8,128)(2,1)S(1)}, u32[]{:S(2)}, u32[]{:S(2)}) collective-permute-start(bf16[1,1,256,12,128]{4,2,3,1,0:T(8,128)(2,1)S(1)} %fusion.75), channel_id=1, source_target_pairs={{4,0},{8,4},{12,8},{5,1},{9,5},{13,9},{6,2},{10,6},{14,10},{7,3},{... | collective-permute-start | bytes 2359304 | tf_op jit(solution)/shard_map/ppermute | solution.py:12
  377.8 10.3 copy-start.12
  377.8 10.3 copy-start.11
  377.8 10.4 copy-start.14
  377.8 10.4 copy-start.13
  377.8 10.4 copy-start.16
  377.8 10.4 copy-start.15
  377.9 10.5 copy-start.18
  377.9 10.5 copy-start.17
  379.3 27.5 %all-to-all-start.8 = ((bf16[1,32,8,12,128]{4,2,3,0,1:T(8,128)(2,1)}), bf16[1,32,8,12,128]{4,2,3,0,1:T(8,128)(2,1)}, u32[]{:S(2)}, u32[]{:S(2)}) async-start(bf16[1,32,8,12,128]{4,2,3,0,1:T(8,128)(2,1)} %copy.187), calls=%async_computation.8 | async-start | bytes 1572864 | tf_op jit(solution)/shard_map/all_to_all | solution.py:71
  410.1 3.1 copy-start.24
  (8 other events, 13.3 us)
where the time goes:
time: 1090 us
  blocking collectives  827 us (76%)
  waiting for transfers between devices  131 us (12%)
  matrix products  62.4 us (6%)
  starting transfers between devices  46.4 us (4%)
  local copies, waits for them, and re-layouts  15.2 us (1%)
    psum x1, blocking collectives, per_device(): gain_total = lax.psum(gain_total, ('seq', 'dp'))  669 us
    all_to_all x3, blocking collectives, per_device(): lax.all_to_all(grad_block, 'seq', split_axis=2, concat_axis=1, tiled=True)  103 us
    all_to_all x2, blocking collectives, per_device(): lax.all_to_all(resid_time, 'seq', split_axis=1, concat_axis=2, tiled=True)  54.6 us
    ppermute x3, waiting for transfers between devices, passed_along(): return lax.ppermute(block, axis, route)  51.8 us
    all_to_all x2, waiting for transfers between devices, per_device(): lax.all_to_all(resid_time, 'seq', split_axis=1, concat_axis=2, tiled=True)  37.6 us
    dot_general x16, matrix products, attend(): jnp.einsum(score_form, query, keys_part, preferred_element_type=jnp.float32)  30.4 us
    dot_general x17, matrix products, attend(): jnp.einsum(mix_form, weights, values.astype(jnp.bfloat16), preferred_elem...  25 us
    all_to_all x1, waiting for transfers between devices, per_device(): lax.all_to_all(mixed_parts, 'seq', split_axis=2, concat_axis=1, tiled=True)  23.3 us
  transfers between devices with their start and end apart: 7, of which 7 were waited for; matrix products, arithmetic and copies ran while one was open for 1% of the time, Pallas kernels for 0%

commit v1 on v0

v1 whole, which is shorter than its diff:
```python
import jax
import jax.numpy as jnp
from jax import lax
from jax.experimental import pallas as pl
from jax.experimental.pallas import tpu as pltpu
from jax.sharding import PartitionSpec as P

MESH = pl.DeviceIdType.MESH
BF = jnp.bfloat16
F32 = jnp.float32
HEADS, HD, TOKENS, FRAMES, SECTIONS = 12, 128, 256, 32, 4
SCALE = HD ** -0.5
EXP2 = SCALE * 1.4426950408889634


def dot(a, b, ca, cb):
    return lax.dot_general(a, b, (((ca,), (cb,)), ((), ())), preferred_element_type=F32)


def attend_fwd(u, gain_q, gain_k, mask):
    r = lax.rsqrt(jnp.mean(u * u, axis=-1, keepdims=True) + 1e-06)
    n = u * r
    q = (n * gain_q).astype(BF)
    k = (n * gain_k).astype(BF)
    st = dot(k, q, 1, 1)
    if mask is not None:
        st = jnp.where(mask, st, -1e30)
    top = jnp.max(st, axis=0, keepdims=True)
    e = jnp.exp2((st - top) * EXP2)
    p = e * (1.0 / jnp.sum(e, axis=0, keepdims=True))
    return r, n, q, k, p


def attend_bwd(do, u, p, pb, q, k, n, r, gain_q, gain_k):
    dp = dot(u, do, 1, 1)
    row = jnp.sum(p * dp, axis=0, keepdims=True)
    ds = (p * (dp - row)).astype(BF)
    du = dot(pb, do, 1, 0)
    dk = dot(ds, q, 1, 0)
    dq = dot(ds, k, 0, 0)
    dn = dq * (gain_q * SCALE) + dk * (gain_k * SCALE)
    along = jnp.mean(dn * n, axis=-1, keepdims=True)
    dx = do.astype(F32) + du + r * (dn - n * along)
    gq = jnp.sum(dq * n, axis=0, keepdims=True) * SCALE
    gk = jnp.sum(dk * n, axis=0, keepdims=True) * SCALE
    return dx, gq, gk


def kernel(a_ref, og_ref, g_ref, out_ref, gout_ref,
           tr, ah, ogh, a_s, og_s, gn, ys, yt, gt, dyt, dys, dxs, outr,
           xf, sp, spb, sq, sk, sn, sr, tx, tp, tpb, tq, tk, tn, trr,
           gsum, ghome, gtot, gbr, gall,
           s_a, r_a, s_og, r_og, s_gn, r_gn, s_y, r_y, s_g, r_g, s_dy, r_dy,
           s_out, r_out, s_p1, r_p1, s_p2, r_p2, s_p3, r_p3):
    seq = lax.axis_index("seq")
    x = lax.axis_index("pipe")
    dp_i = lax.axis_index("dp")
    z_lo, y = seq // 8, seq % 8
    z_hi, c = dp_i // 2, dp_i % 2
    half, yy = y // 4, y % 4
    rest = (yy + 3 - z_lo) % 4
    active = rest < 3
    unit = z_lo + 4 * (3 * half + jnp.minimum(rest, 2))
    u_c, u_h = unit // 12, unit % 12
    d = x * 2 + c

    def dev(xx, y_, zl, zh, cc):
        return {"seq": zl * 8 + y_, "pipe": xx, "dp": zh * 2 + cc}

    def send(src, dst, ssem, rsem, to):
        pltpu.make_async_remote_copy(
            src_ref=src, dst_ref=dst, send_sem=ssem, recv_sem=rsem,
            device_id=to, device_id_type=MESH,
        ).start()

    def copy(src, dst, sem):
        pltpu.make_async_copy(src, dst, sem).start()

    def wait(ref, sem):
        pltpu.make_async_copy(ref, ref, sem).wait()

    def unit_place(cb, h):
        u = cb * 12 + h
        zl, k = u % 4, u // 4
        hf = k // 3
        return hf * 4 + (zl + 1 + k % 3) % 4, zl, hf

    def unit_device(h):
        y_, zl, hf = unit_place(c, h)
        return dev((yy + h) % 4, y_, zl, z_hi, (half + hf + 1 + c) % 2)

    def peer(j):
        p = (d + j) % 8
        return p, dev(p // 2, y, z_lo, z_hi, p % 2)

    def heads_out(src, dst):
        wide = tr.reshape(TOKENS, 16, HD)
        wide[:, 0:HEADS, :] = src[...].astype(F32)
        for h in range(HEADS):
            dst[h] = tr[pl.ds(h, TOKENS, stride=16), :].astype(BF)

    heads_out(a_ref, ah)

    def send_a(h, _):
        send(ah.at[h], a_s.at[x, z_lo], s_a, r_a.at[x], unit_device(h))
        return 0

    lax.fori_loop(0, HEADS, send_a, 0)

    @pl.when(active)
    def _():
        copy(g_ref, gn.at[x], r_gn)

        def send_gain(j, _):
            xx = (x + j) % 4
            send(g_ref, gn.at[x], s_gn, r_gn, dev(xx, y, z_lo, z_hi, c))
            return 0

        lax.fori_loop(1, 4, send_gain, 0)

    heads_out(og_ref, ogh)

    def send_og(m, _):
        h = (x + 4 - yy) % 4 + 4 * m
        send(ogh.at[h], og_s.at[z_lo], s_og, r_og, unit_device(h))
        return 0

    lax.fori_loop(0, 3, send_og, 0)

    gsum[...] = jnp.zeros_like(gsum)

    def to_tokens(src, dst, ssem, rsem):
        copy(src.at[:, pl.ds(pl.multiple_of(d * 32, 32), 32), :], dst.at[d], rsem)

        def one(j, _):
            p, to = peer(j)
            send(src.at[:, pl.ds(pl.multiple_of(p * 32, 32), 32), :], dst.at[d], ssem, rsem, to)
            return 0

        lax.fori_loop(1, 8, one, 0)

    def to_frames(src, dst, ssem, rsem):
        mine = pl.ds(pl.multiple_of(d * 32, 32), 32)
        copy(src.at[d], dst.at[:, mine, :], rsem)

        def one(j, _):
            p, to = peer(j)
            send(src.at[p], dst.at[:, mine, :], ssem, rsem, to)
            return 0

        lax.fori_loop(1, 8, one, 0)

    def gain_row(s, l, j):
        return gn[s, l, j, pl.ds(u_h, 1), :]

    def spatial_fwd(s):
        gq, gk = gain_row(s, 0, 0), gain_row(s, 0, 1)

        def one(i, _):
            ab = a_s[s, i]
            u = ab.astype(F32)
            r, n, q, k, p = attend_fwd(u, gq, gk, None)
            pb = p.astype(BF)
            sp[i] = p
            spb[i] = pb
            sq[i] = q
            sk[i] = k
            sn[i] = n
            sr[i] = jnp.broadcast_to(r, n.shape)
            ys[s, i] = (u + dot(pb, ab, 0, 0)).astype(BF)
            return 0

        lax.fori_loop(0, 4, one, 0, unroll=2)

    def spatial_bwd(s):
        gq, gk = gain_row(s, 0, 0), gain_row(s, 0, 1)

        def one(i, total):
            dx, dgq, dgk = attend_bwd(
                dys[s, i], a_s[s, i], sp[i], spb[i], sq[i], sk[i], sn[i], sr[i], gq, gk)
            dxs[s, i] = dx.astype(BF)
            return total[0] + dgq, total[1] + dgk

        zero = jnp.zeros((1, HD), F32)
        dgq, dgk = lax.fori_loop(0, 4, one, (zero, zero), unroll=2)
        gsum[s, 0:1, :] = dgq
        gsum[s, 1:2, :] = dgk

    ri = lax.broadcasted_iota(jnp.int32, (128, 128), 0)
    ci = lax.broadcasted_iota(jnp.int32, (128, 128), 1)
    same = (ri // 32) == (ci // 32)

    def by_token(src):
        xf[...] = src[...].reshape(FRAMES * 32, HD).astype(F32)

    def token_rows(b):
        return jnp.concatenate(
            [xf[pl.ds(b * 4 + t, FRAMES, stride=32), :] for t in range(4)], axis=0)

    def temporal_fwd(s):
        by_token(yt.at[s])
        gq, gk = gain_row(s, 1, 0), gain_row(s, 1, 1)

        def one(b, _):
            u = token_rows(b)
            r, n, q, k, p = attend_fwd(u, gq, gk, same)
            tx[b] = u.astype(BF)
            tp[b] = p
            tpb[b] = p.astype(BF)
            tq[b] = q
            tk[b] = k
            tn[b] = n
            trr[b] = jnp.broadcast_to(r, n.shape)
            return 0

        lax.fori_loop(0, 8, one, 0, unroll=4)

    def temporal_bwd(s):
        by_token(gt.at[s])
        gq, gk = gain_row(s, 1, 0), gain_row(s, 1, 1)

        def one(b, total):
            do = token_rows(b).astype(BF)
            dx, dgq, dgk = attend_bwd(
                do, tx[b], tp[b], tpb[b], tq[b], tk[b], tn[b], trr[b], gq, gk)
            for t in range(4):
                xf[pl.ds(b * 4 + t, FRAMES, stride=32), :] = dx[t * 32:(t + 1) * 32]
            return total[0] + dgq, total[1] + dgk

        zero = jnp.zeros((1, HD), F32)
        dgq, dgk = lax.fori_loop(0, 8, one, (zero, zero), unroll=4)
        dyt[s] = xf[...].astype(BF).reshape(8, 4, 32, HD)
        gsum[s, 2:3, :] = dgq
        gsum[s, 3:4, :] = dgk

    @pl.when(active)
    def _():
        wait(gn, r_gn)
        last = SECTIONS - 1
        wait(a_s.at[last], r_a.at[last])
        spatial_fwd(last)
        to_tokens(ys.at[last], yt.at[last], s_y.at[last], r_y.at[last])
        wait(og_s, r_og)
        to_tokens(og_s, gt.at[last], s_g.at[last], r_g.at[last])
        wait(yt.at[last], r_y.at[last])
        temporal_fwd(last)

        def section(step, _):
            s = last - step
            before = jnp.maximum(s - 1, 0)
            wait(gt.at[s], r_g.at[s])
            temporal_bwd(s)
            to_frames(dyt.at[s], dys.at[s], s_dy.at[s], r_dy.at[s])
            wait(dys.at[s], r_dy.at[s])
            spatial_bwd(s)

            @pl.when(s > 0)
            def _():
                to_tokens(dxs.at[s], gt.at[before], s_g.at[before], r_g.at[before])

            def send_out(i, _):
                h = u_h
                y4 = (x + 12 - h) % 4
                y_f = y4 + 4 * ((c + half + 1 + u_c) % 2)
                send(dxs.at[s, i], outr.at[h], s_out.at[s], r_out, dev(s, y_f, i, z_hi, u_c))
                return 0

            lax.fori_loop(0, 4, send_out, 0)

            @pl.when(s > 0)
            def _():
                wait(a_s.at[before], r_a.at[before])
                spatial_fwd(before)
                to_tokens(ys.at[before], yt.at[before], s_y.at[before], r_y.at[before])
                wait(yt.at[before], r_y.at[before])
                temporal_fwd(before)

            return 0

        lax.fori_loop(0, SECTIONS, section, 0)

        home = u_h // 2

        def send_home(s, _):
            to = dev(s, home, home % 4, home // 4, u_h % 2)
            at = ghome.at[z_hi, u_c, x, c]
            me_home = ((x == s) & (y == home) & (z_lo == home % 4)
                       & (z_hi == home // 4) & (c == u_h % 2))

            @pl.when(me_home)
            def _():
                copy(gsum.at[s], at, r_p1)

            @pl.when(jnp.logical_not(me_home))
            def _():
                send(gsum.at[s], at, s_p1.at[s], r_p1, to)
                wait(gsum.at[s], s_p1.at[s])

            return 0

        lax.fori_loop(0, SECTIONS, send_home, 0)

    z = z_hi * 4 + z_lo
    is_home = (y < 6) & (z == y)

    @pl.when(is_home)
    def _():
        wait(ghome, r_p1)
        gtot[...] = jnp.sum(ghome[...].reshape(32, 8, HD), axis=0)
        copy(gtot, gbr.at[c], r_p2)

        def spread(j, _):
            e = (z * 2 + c + j) % 16
            ez = e // 2
            send(gtot, gbr.at[c], s_p2.at[j], r_p2, dev(x, y, ez % 4, ez // 4, e % 2))
            return 0

        lax.fori_loop(1, 16, spread, 0)

    @pl.when(y < 6)
    def _():
        wait(gbr, r_p2)
        copy(gbr, gall.at[y], r_p3)

        def along(j, _):
            send(gbr, gall.at[y], s_p3.at[j], r_p3, dev(x, (y + j) % 8, z_lo, z_hi, c))
            return 0

        lax.fori_loop(1, 8, along, 0)

    wait(outr, r_out)
    for h in range(HEADS):
        tr[pl.ds(h, TOKENS, stride=16), :] = outr[h].astype(F32)
    out_ref[...] = tr.reshape(TOKENS, 16, HD)[:, 0:HEADS, :].astype(BF)

    wait(gall, r_p3)
    for h in range(HEADS):
        for l in range(2):
            for j in range(2):
                gout_ref[l, j, h:h + 1, :] = gall[h // 2, h % 2, 2 * l + j:2 * l + j + 1, :]

    wait(ah, s_a)
    wait(ogh.at[pl.ds(0, 3)], s_og)

    @pl.when(active)
    def _():
        wait(gn.at[pl.ds(0, 3)], s_gn)

        def drain(s, _):
            wait(dyt.at[s, pl.ds(0, 7)], s_y.at[s])
            wait(dyt.at[s, pl.ds(0, 7)], s_g.at[s])
            wait(dyt.at[s, pl.ds(0, 7)], s_dy.at[s])
            wait(dxs.at[s], s_out.at[s])
            return 0

        lax.fori_loop(0, SECTIONS, drain, 0)

    @pl.when(is_home)
    def _():
        def drain(j, _):
            wait(gtot, s_p2.at[j])
            return 0

        lax.fori_loop(1, 16, drain, 0)

    @pl.when(y < 6)
    def _():
        def drain(j, _):
            wait(gbr, s_p3.at[j])
            return 0

        lax.fori_loop(1, 8, drain, 0)


def per_device(section_inputs, out_grad, gains):
    a = section_inputs.reshape(TOKENS, HEADS, HD)
    og = out_grad.reshape(TOKENS, HEADS, HD)
    g = gains.reshape(2, 2, HEADS, HD)
    V, D = pltpu.VMEM, pltpu.SemaphoreType.DMA
    s4 = (SECTIONS,)
    scratch = [
        V((TOKENS * 16, HD), F32),
        V((HEADS, TOKENS, HD), BF),
        V((HEADS, TOKENS, HD), BF),
        V((4, 4, TOKENS, HD), BF),
        V((4, TOKENS, HD), BF),
        V((4, 2, 2, HEADS, HD), F32),
        V((4, 4, TOKENS, HD), BF),
        V((4, 8, 4, 32, HD), BF),
        V((4, 8, 4, 32, HD), BF),
        V((4, 8, 4, 32, HD), BF),
        V((4, 4, TOKENS, HD), BF),
        V((4, 4, TOKENS, HD), BF),
        V((HEADS, TOKENS, HD), BF),
        V((FRAMES * 32, HD), F32),
        V((4, TOKENS, TOKENS), F32),
        V((4, TOKENS, TOKENS), BF),
        V((4, TOKENS, HD), BF),
        V((4, TOKENS, HD), BF),
        V((4, TOKENS, HD), F32),
        V((4, TOKENS, HD), F32),
        V((8, 128, HD), BF),
        V((8, 128, 128), F32),
        V((8, 128, 128), BF),
        V((8, 128, HD), BF),
        V((8, 128, HD), BF),
        V((8, 128, HD), F32),
        V((8, 128, HD), F32),
        V((4, 8, HD), F32),
        V((2, 2, 4, 2, 8, HD), F32),
        V((8, HD), F32),
        V((2, 8, HD), F32),
        V((6, 2, 8, HD), F32),
        D, D(s4), D, D, D, D, D(s4), D(s4), D(s4), D(s4), D(s4), D(s4),
        D(s4), D, D(s4), D, D((16,)), D, D((8,)), D,
    ]
    vm = pl.BlockSpec(memory_space=pltpu.VMEM)
    grads, gain_grads = pl.pallas_call(
        kernel,
        out_shape=(
            jax.ShapeDtypeStruct((TOKENS, HEADS, HD), BF),
            jax.ShapeDtypeStruct((2, 2, HEADS, HD), F32),
        ),
        in_specs=[vm, vm, vm],
        out_specs=(vm, vm),
        scratch_shapes=scratch,
        compiler_params=pltpu.CompilerParams(
            has_side_effects=True, vmem_limit_bytes=48 * 1024 * 1024),
        name="sections_back",
    )(a, og, g)
    return grads.reshape(section_inputs.shape), gain_grads[None]


def solution(mesh):
    return jax.shard_map(
        per_device,
        mesh=mesh,
        in_specs=(
            P("pipe", "dp", "seq", None, None, None),
            P("dp", "seq", None, None, None),
            P("pipe", None, None, None, None),
        ),
        out_specs=(P("pipe", "dp", "seq", None, None, None), P("pipe", None, None, None, None)),
        check_vma=False,
    )
```

time: 1090 us -> 181 us (0.17)
  the two profiles are of different devices: /device:TPU:36 before, /device:TPU:1 now
where the time goes in v1:
time: 181 us; the launch traced here: 180 us
  Pallas kernels  175 us (97%)
  local copies, waits for them, and re-layouts  4.74 us (3%)
    pallas_call x1, Pallas kernels, per_device(): pl.pallas_call(kernel, out_shape=(jax.ShapeDtypeStruct((TOKENS, HEADS, HD...  175 us
    unnamed x7, local copies, waits for them, and re-layouts  4.74 us

profile of v1, /device:TPU:1, one launch (start us, length us, event | category | flops | bytes accessed | tf_op | source)
XLA Modules:
  0.0 180.1 jit_solution(2571405398071434487)
XLA Ops:
  0.6 0.7 copy.15
  1.4 0.0 copy-start
  1.4 1.7 copy.14
  3.1 0.0 copy-done
  3.1 0.5 copy.13
  3.7 174.7 %sections_back.1 = (bf16[256,12,128]{2,1,0:T(8,128)(2,1)S(1)}, f32[2,2,12,128]{3,2,1,0:T(8,128)S(1)}) custom-call(bf16[256,12,128]{2,1,0:T(8,128)(2,1)S(1)} %bitcast.11, bf16[256,12,128]{2,1,0:T(8,128)(2,1)S(1)} %bitcast.12, f32[2,2,12,128]{3,2,1,0:T(8,128)S(1)} %bitcast.14), custom_call_target="tpu_custom_call" | custom-call | tf_op jit(solution)/shard_map/sections_back/pallas_call | solution.py:418
  178.4 1.1 copy.8
  179.5 0.6 copy.9
Async XLA Ops:
  1.4 1.8 copy-start

commit v2 on v1

v2 whole, which is shorter than its diff:
```python
import jax
import jax.numpy as jnp
from jax import lax
from jax.experimental import pallas as pl
from jax.experimental.pallas import tpu as pltpu
from jax.sharding import PartitionSpec as P

MESH = pl.DeviceIdType.MESH
BF = jnp.bfloat16
F32 = jnp.float32
HEADS, HD, TOKENS, FRAMES, SECTIONS = 12, 128, 256, 32, 4
SCALE = HD ** -0.5
EXP2 = SCALE * 1.4426950408889634


def dot(a, b, ca, cb):
    return lax.dot_general(a, b, (((ca,), (cb,)), ((), ())), preferred_element_type=F32)


def attend_fwd(u, gain_q, gain_k, mask):
    r = lax.rsqrt(jnp.mean(u * u, axis=-1, keepdims=True) + 1e-06)
    n = u * r
    q = (n * gain_q).astype(BF)
    k = (n * gain_k).astype(BF)
    st = dot(k, q, 1, 1)
    if mask is not None:
        st = jnp.where(mask, st, -1e30)
    top = jnp.max(st, axis=0, keepdims=True)
    e = jnp.exp2((st - top) * EXP2)
    p = e * (1.0 / jnp.sum(e, axis=0, keepdims=True))
    return r, n, q, k, p


def attend_bwd(do, u, p, pb, q, k, n, r, gain_q, gain_k):
    dp = dot(u, do, 1, 1)
    row = jnp.sum(p * dp, axis=0, keepdims=True)
    ds = (p * (dp - row)).astype(BF)
    du = dot(pb, do, 1, 0)
    dk = dot(ds, q, 1, 0)
    dq = dot(ds, k, 0, 0)
    dn = dq * (gain_q * SCALE) + dk * (gain_k * SCALE)
    along = jnp.mean(dn * n, axis=-1, keepdims=True)
    dx = do.astype(F32) + du + r * (dn - n * along)
    gq = jnp.sum(dq * n, axis=0, keepdims=True) * SCALE
    gk = jnp.sum(dk * n, axis=0, keepdims=True) * SCALE
    return dx, gq, gk


def kernel(a_ref, og_ref, g_ref, out_ref, gout_ref,
           l1a, a_s, og_s, gn, ys, yt, gt, dyt, dys, dxs, l1o,
           xf, xo, sp, spb, sq, sk, sn, sr, tx, tp, tpb, tq, tk, tn, trr,
           gsum, gcol, gunit, gl1, gall, gother,
           s_a1, r_a1, s_a2, r_a2, s_og, r_og, s_gn, r_gn, s_y, r_y, s_g, r_g, s_dy, r_dy,
           s_o1, r_o1, s_o2, r_o2, s_p1, r_p1, s_p2, r_p2, s_p3, r_p3, s_p4, r_p4, go):
    seq = lax.axis_index("seq")
    x = lax.axis_index("pipe")
    dp_i = lax.axis_index("dp")
    z_lo, y = seq // 8, seq % 8
    z_hi, c = dp_i // 2, dp_i % 2
    half, yy = y // 4, y % 4
    rest = (yy + 3 - z_lo) % 4
    active = rest < 3
    u_c = half
    u_m = jnp.minimum(rest, 2)
    u_r = (z_lo + 4 - u_m) % 4
    u_h = u_r + 4 * u_m
    d = x * 2 + c
    last = SECTIONS - 1

    def dev(xx, y_, zl, zh, cc):
        return {"seq": zl * 8 + y_, "pipe": xx, "dp": zh * 2 + cc}

    def send(src, dst, ssem, rsem, to):
        pltpu.make_async_remote_copy(
            src_ref=src, dst_ref=dst, send_sem=ssem, recv_sem=rsem,
            device_id=to, device_id_type=MESH,
        ).start()

    def copy(src, dst, sem):
        pltpu.make_async_copy(src, dst, sem).start()

    def wait(ref, sem):
        pltpu.make_async_copy(ref, ref, sem).wait()

    def loop(lo, hi, body):
        def step(i, _):
            body(i)
            return 0

        lax.fori_loop(lo, hi, step, 0)

    def head_row(plane):
        return (plane + 4 - yy + z_lo) % 4

    def unit_device(m):
        zl = (head_row(x) + m) % 4
        return dev(x, 4 * c + (zl + 1 + m) % 4, zl, z_hi, (half + 1) % 2)

    def frame_device(i):
        return dev(x, (x + i + 4 - u_r) % 4 + 4 * ((c + 1) % 2), i, z_hi, u_c)

    def peers():
        for dx in (2, 1, 3, 0):
            for cc in (c, 1 - c) if dx else (1 - c,):
                xx = (x + dx) % 4
                yield xx * 2 + cc, dev(xx, y, z_lo, z_hi, cc)

    def along_x(j):
        xx = (x + j) % 4
        return xx, dev(xx, y, z_lo, z_hi, c)

    samples = [dev(x, y, z_lo, 1 - z_hi, c), dev(x, y, z_lo, 1 - z_hi, 1 - c),
               dev(x, y, z_lo, z_hi, 1 - c)]

    barrier = pltpu.get_barrier_semaphore()

    def greet(to):
        pl.semaphore_signal(barrier, inc=1, device_id=to, device_id_type=MESH)

    for _, to in peers():
        greet(to)
    loop(0, 3, lambda m: greet(unit_device(m)))
    greet(samples[0])
    greet(samples[1])

    @pl.when(active)
    def _():
        loop(0, 4, lambda i: greet(frame_device(i)))
        pl.semaphore_wait(barrier, 16)

    @pl.when(jnp.logical_not(active))
    def _():
        pl.semaphore_wait(barrier, 12)

    def hop_a(m):
        copy(a_ref.at[m, head_row(x)], l1a.at[x, m], r_a1.at[x, m])

        def one(j):
            xx, to = along_x(j)
            send(a_ref.at[m, head_row(xx)], l1a.at[x, m], s_a1, r_a1.at[x, m], to)

        loop(1, 4, one)

    loop(0, 3, lambda j: hop_a((j + z_lo) % 3))
    copy(g_ref, gn.at[x], r_gn)
    loop(1, 4, lambda j: send(g_ref, gn.at[x], s_gn, r_gn, along_x(j)[1]))
    def send_og(j):
        m = (j + z_lo) % 3
        send(og_ref.at[m, head_row(x)], og_s.at[z_lo], s_og, r_og, unit_device(m))

    loop(0, 3, send_og)
    gsum[...] = jnp.zeros_like(gsum)

    def forward_a(s):
        def one(j):
            m = (j + z_lo) % 3
            wait(l1a.at[s, m], r_a1.at[s, m])
            send(l1a.at[s, m], a_s.at[s, z_lo], s_a2.at[s], r_a2.at[s], unit_device(m))

        loop(0, 3, one)

    def hop_out(s):
        row = head_row(x)

        @pl.when(x == s)
        def _():
            def one(m):
                wait(l1o.at[s, m], r_o1.at[s, m])
                copy(l1o.at[s, m], out_ref.at[m, row], r_o2)

            loop(0, 3, one)

        @pl.when(x != s)
        def _():
            def one(m):
                wait(l1o.at[s, m], r_o1.at[s, m])
                send(l1o.at[s, m], out_ref.at[m, row], s_o2.at[s], r_o2, dev(s, y, z_lo, z_hi, c))

            loop(0, 3, one)

    def hop_gains(s):
        row = head_row(x)
        wait(gl1.at[s], r_p2.at[s])

        @pl.when(x == s)
        def _():
            copy(gl1.at[s], gall.at[row], r_p3)

        @pl.when(x != s)
        def _():
            send(gl1.at[s], gall.at[row], s_p3.at[s], r_p3, dev(s, y, z_lo, z_hi, c))

    def share_gains(s):
        copy(gsum.at[s], gcol.at[s, d], r_p1.at[s])
        for _, to in peers():
            send(gsum.at[s], gcol.at[s, d], s_p1.at[s], r_p1.at[s], to)

    def unit_gains(s):
        wait(gcol.at[s], r_p1.at[s])
        gunit[s] = jnp.sum(gcol[s], axis=0)
        loop(0, 4, lambda i: send(
            gunit.at[s], gl1.at[s, u_m], s_p2.at[s], r_p2.at[s], frame_device(i)))

    def send_out(s, lo, hi):
        loop(lo, hi, lambda i: send(
            dxs.at[s, i], l1o.at[s, u_m], s_o1.at[s], r_o1.at[s, u_m],
            frame_device(i)))

    def to_tokens(src, dst, ssem, rsem, first=0, frames=4):
        fr = pl.ds(first, frames)

        def rows(p):
            return src.at[fr, pl.ds(pl.multiple_of(p * 32, 32), 32), :]

        copy(rows(d), dst.at[d, fr], rsem)

        for p, to in peers():
            send(rows(p), dst.at[d, fr], ssem, rsem, to)

    def to_frames(src, dst, ssem, rsem, first):
        mine = pl.ds(pl.multiple_of(d * 32 + first, 16), 16)
        part = pl.ds(first, 16)
        copy(src.at[d, :, part, :], dst.at[:, mine, :], rsem)

        for p, to in peers():
            send(src.at[p, :, part, :], dst.at[:, mine, :], ssem, rsem, to)

    def gain_row(s, l, j):
        return gn[s, l, u_h, j:j + 1, :]

    def spatial_fwd(s):
        gq, gk = gain_row(s, 0, 0), gain_row(s, 0, 1)
        b = s % 2

        def one(i, _):
            ab = a_s[s, i]
            u = ab.astype(F32)
            r, n, q, k, p = attend_fwd(u, gq, gk, None)
            pb = p.astype(BF)
            sp[b, i] = p
            spb[b, i] = pb
            sq[b, i] = q
            sk[b, i] = k
            sn[b, i] = n
            sr[b, i] = jnp.broadcast_to(r, n.shape)
            ys[s, i] = (u + dot(pb, ab, 0, 0)).astype(BF)
            return 0

        lax.fori_loop(0, 4, one, 0, unroll=2)

    def add_gains(s, l, dgq, dgk):
        gsum[s, 2 * l:2 * l + 1, :] += dgq
        gsum[s, 2 * l + 1:2 * l + 2, :] += dgk

    def spatial_bwd(s, first):
        gq, gk = gain_row(s, 0, 0), gain_row(s, 0, 1)
        b = s % 2
        for i in (first, first + 1):
            dx, dgq, dgk = attend_bwd(
                dys[s, i], a_s[s, i], sp[b, i], spb[b, i], sq[b, i], sk[b, i], sn[b, i],
                sr[b, i], gq, gk)
            dxs[s, i] = dx.astype(BF)
            add_gains(s, 0, dgq, dgk)

    ri = lax.broadcasted_iota(jnp.int32, (128, 128), 0)
    ci = lax.broadcasted_iota(jnp.int32, (128, 128), 1)
    same = (ri // 32) == (ci // 32)

    def by_token(src):
        xf[...] = src[...].reshape(FRAMES * 32, HD).astype(F32)

    def token_rows(b):
        return jnp.concatenate(
            [xf[pl.ds(b * 4 + t, FRAMES, stride=32), :] for t in range(4)], axis=0)

    def temporal_fwd(s):
        by_token(yt.at[s])
        gq, gk = gain_row(s, 1, 0), gain_row(s, 1, 1)
        for b in range(8):
            u = token_rows(b)
            r, n, q, k, p = attend_fwd(u, gq, gk, same)
            tx[b] = u.astype(BF)
            tp[b] = p
            tpb[b] = p.astype(BF)
            tq[b] = q
            tk[b] = k
            tn[b] = n
            trr[b] = jnp.broadcast_to(r, n.shape)

    def temporal_bwd(s, first):
        gq, gk = gain_row(s, 1, 0), gain_row(s, 1, 1)
        for b in range(first, first + 4):
            dx, dgq, dgk = attend_bwd(
                token_rows(b).astype(BF), tx[b], tp[b], tpb[b], tq[b], tk[b], tn[b], trr[b],
                gq, gk)
            for t in range(4):
                xo[pl.ds(b * 4 + t, FRAMES, stride=32), :] = dx[t * 32:(t + 1) * 32]
            add_gains(s, 1, dgq, dgk)
        part = slice(4 * first, 4 * first + 16)
        dyt[s, :, :, part, :] = xo.reshape(8, 4, 32, HD)[:, :, part, :].astype(BF)

    forward_a(last)

    @pl.when(active)
    def _():
        wait(og_s, r_og)
        to_tokens(og_s, gt.at[last], s_g.at[last], r_g.at[last])
        wait(gn, r_gn)
        wait(a_s.at[last], r_a2.at[last])
        spatial_fwd(last)
        to_tokens(ys.at[last], yt.at[last], s_y.at[last], r_y.at[last])
        loop(0, 4, lambda i: pl.semaphore_signal(
            go, inc=1, device_id=frame_device(i), device_id_type=MESH))
        forward_a(last - 1)
        wait(yt.at[last], r_y.at[last])
        temporal_fwd(last)

        def section(step):
            s = last - step
            before = jnp.maximum(s - 1, 0)
            after = jnp.minimum(s + 1, last)
            wait(gt.at[s], r_g.at[s])
            by_token(gt.at[s])
            for part in range(2):
                temporal_bwd(s, 4 * part)
                to_frames(dyt.at[s], dys.at[s], s_dy.at[s], r_dy.at[s], 16 * part)

            @pl.when(s == last)
            def _():
                forward_a(1)
                forward_a(0)

            @pl.when(s > 0)
            def _():
                wait(a_s.at[before], r_a2.at[before])
                spatial_fwd(before)
                to_tokens(ys.at[before], yt.at[before], s_y.at[before], r_y.at[before])

            @pl.when(s < last)
            def _():
                unit_gains(after)

            wait(dys.at[s], r_dy.at[s])

            @pl.when(s == 0)
            def _():
                hop_out(3)

            for part in range(2):
                spatial_bwd(s, 2 * part)

                @pl.when(s > 0)
                def _():
                    to_tokens(dxs.at[s], gt.at[before], s_g.at[before], r_g.at[before],
                              2 * part, 2)

                @pl.when(s == 0)
                def _():
                    send_out(s, 2 * part, 2 * part + 2)

            @pl.when(s > 0)
            def _():
                wait(yt.at[before], r_y.at[before])
                temporal_fwd(before)
                send_out(s, 0, 4)

            share_gains(s)

        loop(0, SECTIONS, section)
        hop_out(2)
        hop_out(1)
        pl.semaphore_wait(go, 3)
        loop(0, SECTIONS - 1, lambda j: hop_gains(last - j))
        unit_gains(0)

    @pl.when(jnp.logical_not(active))
    def _():
        wait(gn, r_gn)
        pl.semaphore_wait(go, 3)
        loop(1, SECTIONS, lambda j: forward_a(last - j))

        def relay(j):
            hop_out(last - j)
            hop_gains(last - j)

        loop(0, SECTIONS - 1, relay)

    hop_out(0)
    hop_gains(0)

    wait(gall, r_p3)
    for j, to in enumerate(samples):
        send(gall, gother.at[j], s_p4, r_p4, to)
    wait(gother, r_p4)
    for row in range(4):
        for m in range(3):
            total = gall[row, m] + (gother[0, row, m] + gother[1, row, m] + gother[2, row, m])
            for l in range(2):
                gout_ref[l, row + 4 * m] = total[2 * l:2 * l + 2]

    wait(out_ref, r_o2)

    wait(l1a.at[pl.ds(0, 3)], s_a1)
    wait(og_s.at[pl.ds(0, 3)], s_og)
    wait(gn.at[pl.ds(0, 3)], s_gn)
    wait(gother, s_p4)

    def drain(s):
        wait(l1a.at[s], s_a2.at[s])

        @pl.when(x != s)
        def _():
            wait(l1o.at[s], s_o2.at[s])
            wait(gl1.at[s], s_p3.at[s])

    loop(0, SECTIONS, drain)

    @pl.when(active)
    def _():
        def drain(s):
            wait(dyt.at[s, pl.ds(0, 7)], s_y.at[s])
            wait(dyt.at[s, pl.ds(0, 7)], s_g.at[s])
            wait(dyt.at[s, pl.ds(0, 7)], s_dy.at[s])
            wait(dxs.at[s], s_o1.at[s])
            wait(gcol.at[s, pl.ds(0, 7)], s_p1.at[s])
            wait(gcol.at[s, pl.ds(0, 4)], s_p2.at[s])

        loop(0, SECTIONS, drain)


def per_device(section_inputs, out_grad, gains):
    def by_head(block):
        return block.reshape(TOKENS, HEADS, HD).transpose(1, 0, 2).reshape(3, 4, TOKENS, HD)

    a, og = by_head(section_inputs), by_head(out_grad)
    g = gains.reshape(2, 2, HEADS, HD).transpose(0, 2, 1, 3)
    V, D = pltpu.VMEM, pltpu.SemaphoreType.DMA
    s4, s43 = (SECTIONS,), (SECTIONS, 3)
    scratch = [
        V((4, 3, TOKENS, HD), BF),
        V((4, 4, TOKENS, HD), BF),
        V((4, TOKENS, HD), BF),
        V((4, 2, HEADS, 2, HD), F32),
        V((4, 4, TOKENS, HD), BF),
        V((4, 8, 4, 32, HD), BF),
        V((4, 8, 4, 32, HD), BF),
        V((4, 8, 4, 32, HD), BF),
        V((4, 4, TOKENS, HD), BF),
        V((4, 4, TOKENS, HD), BF),
        V((4, 3, TOKENS, HD), BF),
        V((FRAMES * 32, HD), F32),
        V((FRAMES * 32, HD), F32),
        V((2, 4, TOKENS, TOKENS), F32),
        V((2, 4, TOKENS, TOKENS), BF),
        V((2, 4, TOKENS, HD), BF),
        V((2, 4, TOKENS, HD), BF),
        V((2, 4, TOKENS, HD), F32),
        V((2, 4, TOKENS, HD), F32),
        V((8, 128, HD), BF),
        V((8, 128, 128), F32),
        V((8, 128, 128), BF),
        V((8, 128, HD), BF),
        V((8, 128, HD), BF),
        V((8, 128, HD), F32),
        V((8, 128, HD), F32),
        V((4, 4, HD), F32),
        V((4, 8, 4, HD), F32),
        V((4, 4, HD), F32),
        V((4, 3, 4, HD), F32),
        V((4, 3, 4, HD), F32),
        V((3, 4, 3, 4, HD), F32),
        D, D(s43), D(s4), D(s4), D, D, D, D, D(s4), D(s4), D(s4), D(s4), D(s4), D(s4),
        D(s4), D(s43), D(s4), D, D(s4), D(s4), D(s4), D(s4), D(s4), D, D, D, pltpu.SemaphoreType.REGULAR,
    ]
    vm = pl.BlockSpec(memory_space=pltpu.VMEM)
    hbm = pl.BlockSpec(memory_space=pltpu.HBM)
    grads, gain_grads = pl.pallas_call(
        kernel,
        out_shape=(
            jax.ShapeDtypeStruct((3, 4, TOKENS, HD), BF),
            jax.ShapeDtypeStruct((2, HEADS, 2, HD), F32),
        ),
        in_specs=[hbm, hbm, hbm],
        out_specs=(vm, vm),
        scratch_shapes=scratch,
        compiler_params=pltpu.CompilerParams(
            has_side_effects=True, collective_id=0, vmem_limit_bytes=40 * 1024 * 1024),
        name="sections_back",
    )(a, og, g)
    grads = grads.reshape(HEADS, TOKENS, HD).transpose(1, 0, 2).reshape(section_inputs.shape)
    return grads, gain_grads.transpose(0, 2, 1, 3)[None]


def solution(mesh):
    return jax.shard_map(
        per_device,
        mesh=mesh,
        in_specs=(
            P("pipe", "dp", "seq", None, None, None),
            P("dp", "seq", None, None, None),
            P("pipe", None, None, None, None),
        ),
        out_specs=(P("pipe", "dp", "seq", None, None, None), P("pipe", None, None, None, None)),
        check_vma=False,
    )
```

time: 181 us -> 117 us (0.65)
  Pallas kernels: 175 us -> 111 us
    pallas_call x1, Pallas kernels: 175 us -> 111 us  [per_device(): pl.pallas_call(kernel, out_shape=(jax.ShapeDtypeStruct((3, 4, TOKENS, HD)...]
    unnamed x7 -> x8, local copies, waits for them, and re-layouts: 4.74 us -> 4.49 us
where the time goes in v2:
time: 117 us
  Pallas kernels  111 us (95%)
  local copies, waits for them, and re-layouts  4.49 us (4%)
    pallas_call x1, Pallas kernels, per_device(): pl.pallas_call(kernel, out_shape=(jax.ShapeDtypeStruct((3, 4, TOKENS, HD)...  111 us
    unnamed x8, local copies, waits for them, and re-layouts  4.49 us

profile of v2, /device:TPU:1, one launch (start us, length us, event | category | flops | bytes accessed | tf_op | source)
XLA Modules:
  0.0 116.6 jit_solution(13061706903275006951)
XLA Ops:
  0.6 0.0 copy-start
  0.6 1.1 copy-done
  1.8 0.0 copy-start.1
  1.8 1.1 copy-done.1
  2.9 0.0 copy-start.2
  2.9 0.7 copy-done.2
  3.6 111.5 %sections_back.1 = (bf16[3,4,256,128]{3,2,1,0:T(8,128)(2,1)S(1)}, f32[2,12,2,128]{3,2,1,0:T(2,128)S(1)}) custom-call(bf16[3,4,256,128]{3,2,1,0:T(8,128)(2,1)S(1)} %bitcast.21, bf16[3,4,256,128]{3,2,1,0:T(8,128)(2,1)S(1)} %bitcast.22, f32[2,12,2,128]{3,2,1,0:T(2,128)S(1)} %bitcast.25), custom_call_target="tpu_custom_call" | custom-call | tf_op jit(solution)/shard_map/sections_back/pallas_call | solution.py:477
  115.1 0.9 copy.7
  116.0 0.6 copy.8
Async XLA Ops:
  0.6 1.1 copy-start
  1.8 1.1 copy-start.1
  2.9 0.7 copy-start.2

commit v3 on v2

--- a/solution.py
+++ b/solution.py
@@ -17,41 +17,46 @@
     return lax.dot_general(a, b, (((ca,), (cb,)), ((), ())), preferred_element_type=F32)
 
 
-def attend_fwd(u, gain_q, gain_k, mask):
-    r = lax.rsqrt(jnp.mean(u * u, axis=-1, keepdims=True) + 1e-06)
-    n = u * r
-    q = (n * gain_q).astype(BF)
-    k = (n * gain_k).astype(BF)
-    st = dot(k, q, 1, 1)
-    if mask is not None:
-        st = jnp.where(mask, st, -1e30)
-    top = jnp.max(st, axis=0, keepdims=True)
-    e = jnp.exp2((st - top) * EXP2)
-    p = e * (1.0 / jnp.sum(e, axis=0, keepdims=True))
-    return r, n, q, k, p
-
-
-def attend_bwd(do, u, p, pb, q, k, n, r, gain_q, gain_k):
-    dp = dot(u, do, 1, 1)
-    row = jnp.sum(p * dp, axis=0, keepdims=True)
-    ds = (p * (dp - row)).astype(BF)
-    du = dot(pb, do, 1, 0)
-    dk = dot(ds, q, 1, 0)
-    dq = dot(ds, k, 0, 0)
-    dn = dq * (gain_q * SCALE) + dk * (gain_k * SCALE)
-    along = jnp.mean(dn * n, axis=-1, keepdims=True)
-    dx = do.astype(F32) + du + r * (dn - n * along)
-    gq = jnp.sum(dq * n, axis=0, keepdims=True) * SCALE
-    gk = jnp.sum(dk * n, axis=0, keepdims=True) * SCALE
-    return dx, gq, gk
+def attend_fwd(us, gain_q, gain_k, mask):
+    rs = [lax.rsqrt(jnp.mean(u * u, axis=-1, keepdims=True) + 1e-06) for u in us]
+    ns = [u * r for u, r in zip(us, rs)]
+    qs = [(n * gain_q).astype(BF) for n in ns]
+    ks = [(n * gain_k).astype(BF) for n in ns]
+    ps = []
+    for st in [dot(k, q, 1, 1) for k, q in zip(ks, qs)]:
+        if mask is not None:
+            st = jnp.where(mask, st, -1e30)
+        top = jnp.max(st, axis=0, keepdims=True)
+        e = jnp.exp2((st - top) * EXP2)
+        ps.append(e * (1.0 / jnp.sum(e, axis=0, keepdims=True)))
+    return rs, ns, qs, ks, ps
+
+
+def attend_bwd(blocks, gain_q, gain_k):
+    dps = [dot(u, do, 1, 1) for do, u, p, pb, q, k, n, r in blocks]
+    dus = [dot(pb, do, 1, 0) for do, u, p, pb, q, k, n, r in blocks]
+    dss = []
+    for dp, (do, u, p, pb, q, k, n, r) in zip(dps, blocks):
+        row = jnp.sum(p * dp, axis=0, keepdims=True)
+        dss.append((p * (dp - row)).astype(BF))
+    dks = [dot(ds, b[4], 1, 0) for ds, b in zip(dss, blocks)]
+    dqs = [dot(ds, b[5], 0, 0) for ds, b in zip(dss, blocks)]
+    dxs, gq, gk = [], 0.0, 0.0
+    for dk, dq, du, (do, u, p, pb, q, k, n, r) in zip(dks, dqs, dus, blocks):
+        dn = dq * (gain_q * SCALE) + dk * (gain_k * SCALE)
+        along = jnp.mean(dn * n, axis=-1, keepdims=True)
+        dxs.append(do.astype(F32) + du + r * (dn - n * along))
+        gq = gq + jnp.sum(dq * n, axis=0, keepdims=True)
+        gk = gk + jnp.sum(dk * n, axis=0, keepdims=True)
+    return dxs, gq * SCALE, gk * SCALE
 
 
 def kernel(a_ref, og_ref, g_ref, out_ref, gout_ref,
            l1a, a_s, og_s, gn, ys, yt, gt, dyt, dys, dxs, l1o,
            xf, xo, sp, spb, sq, sk, sn, sr, tx, tp, tpb, tq, tk, tn, trr,
-           gsum, gcol, gunit, gl1, gall, gother,
+           gsum, gcol, gunit, gl1, ghop, gall,
            s_a1, r_a1, s_a2, r_a2, s_og, r_og, s_gn, r_gn, s_y, r_y, s_g, r_g, s_dy, r_dy,
-           s_o1, r_o1, s_o2, r_o2, s_p1, r_p1, s_p2, r_p2, s_p3, r_p3, s_p4, r_p4, go):
+           s_o1, r_o1, s_o2, r_o2, s_p1, r_p1, s_p2, r_p2, s_p3, r_p3, go):
     seq = lax.axis_index("seq")
     x = lax.axis_index("pipe")
     dp_i = lax.axis_index("dp")
@@ -109,8 +114,17 @@
         xx = (x + j) % 4
         return xx, dev(xx, y, z_lo, z_hi, c)
 
-    samples = [dev(x, y, z_lo, 1 - z_hi, c), dev(x, y, z_lo, 1 - z_hi, 1 - c),
-               dev(x, y, z_lo, z_hi, 1 - c)]
+    def sample_units(m):
+        zl = (head_row(x) + m) % 4
+        for zh in range(2):
+            for cc in range(2):
+                yield dev(x, 4 * cc + (zl + 1 + m) % 4, zl, zh, (half + 1) % 2)
+
+    def sample_frames(i):
+        y_f = (x + i + 4 - u_r) % 4 + 4 * ((c + 1) % 2)
+        for zh in range(2):
+            for cc in range(2):
+                yield dev(x, y_f, i, zh, cc)
 
     barrier = pltpu.get_barrier_semaphore()
 
@@ -119,18 +133,34 @@
 
     for _, to in peers():
         greet(to)
-    loop(0, 3, lambda m: greet(unit_device(m)))
-    greet(samples[0])
-    greet(samples[1])
+
+    def is_me(to):
+        return (to["seq"] == seq) & (to["dp"] == dp_i)
+
+    own = active & ((x + z_lo + 4 - u_r) % 4 + 4 * ((c + 1) % 2) == y)
+
+    def greet_all(devices):
+        for to in devices:
+            @pl.when(jnp.logical_not(is_me(to)))
+            def _():
+                greet(to)
+
+    loop(0, 3, lambda m: greet_all(sample_units(m)))
 
     @pl.when(active)
     def _():
-        loop(0, 4, lambda i: greet(frame_device(i)))
-        pl.semaphore_wait(barrier, 16)
+        loop(0, 4, lambda i: greet_all(sample_frames(i)))
+        @pl.when(own)
+        def _():
+            pl.semaphore_wait(barrier, 33)
+
+        @pl.when(jnp.logical_not(own))
+        def _():
+            pl.semaphore_wait(barrier, 35)
 
     @pl.when(jnp.logical_not(active))
     def _():
-        pl.semaphore_wait(barrier, 12)
+        pl.semaphore_wait(barrier, 19)
 
     def hop_a(m):
         copy(a_ref.at[m, head_row(x)], l1a.at[x, m], r_a1.at[x, m])
@@ -141,7 +171,11 @@
 
         loop(1, 4, one)
 
-    loop(0, 3, lambda j: hop_a((j + z_lo) % 3))
+    def hops_a():
+        loop(0, 3, lambda j: hop_a((j + z_lo) % 3))
+
+    hops_a()
+
     copy(g_ref, gn.at[x], r_gn)
     loop(1, 4, lambda j: send(g_ref, gn.at[x], s_gn, r_gn, along_x(j)[1]))
     def send_og(j):
@@ -159,7 +193,7 @@
 
         loop(0, 3, one)
 
-    def hop_out(s):
+    def hop_out(s, lo=0, hi=3):
         row = head_row(x)
 
         @pl.when(x == s)
@@ -168,7 +202,7 @@
                 wait(l1o.at[s, m], r_o1.at[s, m])
                 copy(l1o.at[s, m], out_ref.at[m, row], r_o2)
 
-            loop(0, 3, one)
+            loop(lo, hi, one)
 
         @pl.when(x != s)
         def _():
@@ -176,19 +210,20 @@
                 wait(l1o.at[s, m], r_o1.at[s, m])
                 send(l1o.at[s, m], out_ref.at[m, row], s_o2.at[s], r_o2, dev(s, y, z_lo, z_hi, c))
 
-            loop(0, 3, one)
+            loop(lo, hi, one)
 
     def hop_gains(s):
         row = head_row(x)
         wait(gl1.at[s], r_p2.at[s])
+        ghop[s] = jnp.sum(gl1[s], axis=1)
 
         @pl.when(x == s)
         def _():
-            copy(gl1.at[s], gall.at[row], r_p3)
+            copy(ghop.at[s], gall.at[row], r_p3)
 
         @pl.when(x != s)
         def _():
-            send(gl1.at[s], gall.at[row], s_p3.at[s], r_p3, dev(s, y, z_lo, z_hi, c))
+            send(ghop.at[s], gall.at[row], s_p3.at[s], r_p3, dev(s, y, z_lo, z_hi, c))
 
     def share_gains(s):
         copy(gsum.at[s], gcol.at[s, d], r_p1.at[s])
@@ -198,8 +233,19 @@
     def unit_gains(s):
         wait(gcol.at[s], r_p1.at[s])
         gunit[s] = jnp.sum(gcol[s], axis=0)
-        loop(0, 4, lambda i: send(
-            gunit.at[s], gl1.at[s, u_m], s_p2.at[s], r_p2.at[s], frame_device(i)))
+
+        def one(i):
+            at = gl1.at[s, u_m, z_hi * 2 + u_c]
+            for to in sample_frames(i):
+                @pl.when(is_me(to))
+                def _():
+                    copy(gunit.at[s], at, r_p2.at[s])
+
+                @pl.when(jnp.logical_not(is_me(to)))
+                def _():
+                    send(gunit.at[s], at, s_p2.at[s], r_p2.at[s], to)
+
+        loop(0, 4, one)
 
     def send_out(s, lo, hi):
         loop(lo, hi, lambda i: send(
@@ -231,11 +277,10 @@
     def spatial_fwd(s):
         gq, gk = gain_row(s, 0, 0), gain_row(s, 0, 1)
         b = s % 2
-
-        def one(i, _):
+        for i in range(4):
             ab = a_s[s, i]
             u = ab.astype(F32)
-            r, n, q, k, p = attend_fwd(u, gq, gk, None)
+            (r,), (n,), (q,), (k,), (p,) = attend_fwd([u], gq, gk, None)
             pb = p.astype(BF)
             sp[b, i] = p
             spb[b, i] = pb
@@ -244,9 +289,6 @@
             sn[b, i] = n
             sr[b, i] = jnp.broadcast_to(r, n.shape)
             ys[s, i] = (u + dot(pb, ab, 0, 0)).astype(BF)
-            return 0
-
-        lax.fori_loop(0, 4, one, 0, unroll=2)
 
     def add_gains(s, l, dgq, dgk):
         gsum[s, 2 * l:2 * l + 1, :] += dgq
@@ -255,12 +297,13 @@
     def spatial_bwd(s, first):
         gq, gk = gain_row(s, 0, 0), gain_row(s, 0, 1)
         b = s % 2
-        for i in (first, first + 1):
-            dx, dgq, dgk = attend_bwd(
-                dys[s, i], a_s[s, i], sp[b, i], spb[b, i], sq[b, i], sk[b, i], sn[b, i],
-                sr[b, i], gq, gk)
-            dxs[s, i] = dx.astype(BF)
-            add_gains(s, 0, dgq, dgk)
+        two = (first, first + 1)
+        dx, dgq, dgk = attend_bwd(
+            [(dys[s, i], a_s[s, i], sp[b, i], spb[b, i], sq[b, i], sk[b, i], sn[b, i], sr[b, i])
+             for i in two], gq, gk)
+        for i, block in zip(two, dx):
+            dxs[s, i] = block.astype(BF)
+        add_gains(s, 0, dgq, dgk)
 
     ri = lax.broadcasted_iota(jnp.int32, (128, 128), 0)
     ci = lax.broadcasted_iota(jnp.int32, (128, 128), 1)
@@ -276,26 +319,28 @@
     def temporal_fwd(s):
         by_token(yt.at[s])
         gq, gk = gain_row(s, 1, 0), gain_row(s, 1, 1)
-        for b in range(8):
-            u = token_rows(b)
-            r, n, q, k, p = attend_fwd(u, gq, gk, same)
-            tx[b] = u.astype(BF)
-            tp[b] = p
-            tpb[b] = p.astype(BF)
-            tq[b] = q
-            tk[b] = k
-            tn[b] = n
-            trr[b] = jnp.broadcast_to(r, n.shape)
+        for first in range(0, 8, 4):
+            four = range(first, first + 4)
+            us = [token_rows(b) for b in four]
+            for b, u, r, n, q, k, p in zip(four, us, *attend_fwd(us, gq, gk, same)):
+                tx[b] = u.astype(BF)
+                tp[b] = p
+                tpb[b] = p.astype(BF)
+                tq[b] = q
+                tk[b] = k
+                tn[b] = n
+                trr[b] = jnp.broadcast_to(r, n.shape)
 
     def temporal_bwd(s, first):
         gq, gk = gain_row(s, 1, 0), gain_row(s, 1, 1)
-        for b in range(first, first + 4):
-            dx, dgq, dgk = attend_bwd(
-                token_rows(b).astype(BF), tx[b], tp[b], tpb[b], tq[b], tk[b], tn[b], trr[b],
-                gq, gk)
+        four = range(first, first + 4)
+        dx, dgq, dgk = attend_bwd(
+            [(token_rows(b).astype(BF), tx[b], tp[b], tpb[b], tq[b], tk[b], tn[b], trr[b])
+             for b in four], gq, gk)
+        for b, block in zip(four, dx):
             for t in range(4):
-                xo[pl.ds(b * 4 + t, FRAMES, stride=32), :] = dx[t * 32:(t + 1) * 32]
-            add_gains(s, 1, dgq, dgk)
+                xo[pl.ds(b * 4 + t, FRAMES, stride=32), :] = block[t * 32:(t + 1) * 32]
+        add_gains(s, 1, dgq, dgk)
         part = slice(4 * first, 4 * first + 16)
         dyt[s, :, :, part, :] = xo.reshape(8, 4, 32, HD)[:, :, part, :].astype(BF)
 
@@ -325,10 +370,9 @@
                 temporal_bwd(s, 4 * part)
                 to_frames(dyt.at[s], dys.at[s], s_dy.at[s], r_dy.at[s], 16 * part)
 
-            @pl.when(s == last)
-            def _():
-                forward_a(1)
-                forward_a(0)
+            @pl.when(s > 1)
+            def _():
+                forward_a(jnp.maximum(s - 2, 0))
 
             @pl.when(s > 0)
             def _():
@@ -344,34 +388,44 @@
 
             @pl.when(s == 0)
             def _():
-                hop_out(3)
-
-            for part in range(2):
-                spatial_bwd(s, 2 * part)
-
-                @pl.when(s > 0)
-                def _():
-                    to_tokens(dxs.at[s], gt.at[before], s_g.at[before], r_g.at[before],
-                              2 * part, 2)
-
-                @pl.when(s == 0)
-                def _():
-                    send_out(s, 2 * part, 2 * part + 2)
+                hop_gains(3)
+                hop_gains(2)
+
+            spatial_bwd(s, 0)
 
             @pl.when(s > 0)
             def _():
+                to_tokens(dxs.at[s], gt.at[before], s_g.at[before], r_g.at[before], 0, 2)
+
+            @pl.when(s == 0)
+            def _():
+                send_out(s, 0, 2)
+
+            spatial_bwd(s, 2)
+
+            @pl.when(s > 0)
+            def _():
+                to_tokens(dxs.at[s], gt.at[before], s_g.at[before], r_g.at[before], 2, 2)
                 wait(yt.at[before], r_y.at[before])
                 temporal_fwd(before)
+
+            share_gains(s)
+
+            @pl.when(s > 0)
+            def _():
                 send_out(s, 0, 4)
 
-            share_gains(s)
+            @pl.when(s == 0)
+            def _():
+                send_out(s, 2, 4)
 
         loop(0, SECTIONS, section)
+        pl.semaphore_wait(go, 3)
+        unit_gains(0)
+        hop_gains(1)
+        hop_out(3)
         hop_out(2)
         hop_out(1)
-        pl.semaphore_wait(go, 3)
-        loop(0, SECTIONS - 1, lambda j: hop_gains(last - j))
-        unit_gains(0)
 
     @pl.when(jnp.logical_not(active))
     def _():
@@ -389,21 +443,16 @@
     hop_gains(0)
 
     wait(gall, r_p3)
-    for j, to in enumerate(samples):
-        send(gall, gother.at[j], s_p4, r_p4, to)
-    wait(gother, r_p4)
     for row in range(4):
         for m in range(3):
-            total = gall[row, m] + (gother[0, row, m] + gother[1, row, m] + gother[2, row, m])
             for l in range(2):
-                gout_ref[l, row + 4 * m] = total[2 * l:2 * l + 2]
+                gout_ref[l, row + 4 * m] = gall[row, m, 2 * l:2 * l + 2]
 
     wait(out_ref, r_o2)
 
     wait(l1a.at[pl.ds(0, 3)], s_a1)
     wait(og_s.at[pl.ds(0, 3)], s_og)
     wait(gn.at[pl.ds(0, 3)], s_gn)
-    wait(gother, s_p4)
 
     def drain(s):
         wait(l1a.at[s], s_a2.at[s])
@@ -411,21 +460,44 @@
         @pl.when(x != s)
         def _():
             wait(l1o.at[s], s_o2.at[s])
-            wait(gl1.at[s], s_p3.at[s])
+            wait(ghop.at[s], s_p3.at[s])
 
     loop(0, SECTIONS, drain)
 
     @pl.when(active)
     def _():
+        slots = gcol.reshape(32, 4, HD)
+
         def drain(s):
             wait(dyt.at[s, pl.ds(0, 7)], s_y.at[s])
             wait(dyt.at[s, pl.ds(0, 7)], s_g.at[s])
             wait(dyt.at[s, pl.ds(0, 7)], s_dy.at[s])
             wait(dxs.at[s], s_o1.at[s])
             wait(gcol.at[s, pl.ds(0, 7)], s_p1.at[s])
-            wait(gcol.at[s, pl.ds(0, 4)], s_p2.at[s])
+
+            @pl.when(own)
+            def _():
+                wait(slots.at[pl.ds(0, 15)], s_p2.at[s])
+
+            @pl.when(jnp.logical_not(own))
+            def _():
+                wait(slots.at[pl.ds(0, 16)], s_p2.at[s])
 
         loop(0, SECTIONS, drain)
+
+
+def hand_over(grads, gains, grads_out, gains_out, buf, gbuf, s_in, s_out):
+    parts = [(grads.at[m], buf.at[m], grads_out.at[m]) for m in range(3)]
+    parts.append((gains, gbuf, gains_out))
+    first = [pltpu.make_async_copy(a, b, s_in.at[i]) for i, (a, b, _) in enumerate(parts)]
+    second = [pltpu.make_async_copy(b, c, s_out.at[i]) for i, (_, b, c) in enumerate(parts)]
+    for one in first:
+        one.start()
+    for one, other in zip(first, second):
+        one.wait()
+        other.start()
+    for one in second:
+        one.wait()
 
 
 def per_device(section_inputs, out_grad, gains):
@@ -466,14 +538,14 @@
         V((4, 4, HD), F32),
         V((4, 8, 4, HD), F32),
         V((4, 4, HD), F32),
+        V((4, 3, 4, 4, HD), F32),
         V((4, 3, 4, HD), F32),
         V((4, 3, 4, HD), F32),
-        V((3, 4, 3, 4, HD), F32),
         D, D(s43), D(s4), D(s4), D, D, D, D, D(s4), D(s4), D(s4), D(s4), D(s4), D(s4),
-        D(s4), D(s43), D(s4), D, D(s4), D(s4), D(s4), D(s4), D(s4), D, D, D, pltpu.SemaphoreType.REGULAR,
+        D(s4), D(s43), D(s4), D, D(s4), D(s4), D(s4), D(s4), D(s4), D, pltpu.SemaphoreType.REGULAR,
     ]
     vm = pl.BlockSpec(memory_space=pltpu.VMEM)
-    hbm = pl.BlockSpec(memory_space=pltpu.HBM)
+    hbm = pl.BlockSpec(memory_space=pl.ANY)
     grads, gain_grads = pl.pallas_call(
         kernel,
         out_shape=(
@@ -481,12 +553,24 @@
             jax.ShapeDtypeStruct((2, HEADS, 2, HD), F32),
         ),
         in_specs=[hbm, hbm, hbm],
-        out_specs=(vm, vm),
+        out_specs=(hbm, vm),
         scratch_shapes=scratch,
         compiler_params=pltpu.CompilerParams(
-            has_side_effects=True, collective_id=0, vmem_limit_bytes=40 * 1024 * 1024),
+            has_side_effects=True, collective_id=0, vmem_limit_bytes=60 * 1024 * 1024),
         name="sections_back",
     )(a, og, g)
+    grads, gain_grads = pl.pallas_call(
+        hand_over,
+        out_shape=(
+            jax.ShapeDtypeStruct(grads.shape, BF),
+            jax.ShapeDtypeStruct(gain_grads.shape, F32),
+        ),
+        in_specs=[hbm, hbm],
+        out_specs=(hbm, hbm),
+        scratch_shapes=[V(grads.shape, BF), V(gain_grads.shape, F32), D(s4), D(s4)],
+        compiler_params=pltpu.CompilerParams(vmem_limit_bytes=60 * 1024 * 1024),
+        name="hand_over",
+    )(grads, gain_grads)
     grads = grads.reshape(HEADS, TOKENS, HD).transpose(1, 0, 2).reshape(section_inputs.shape)
     return grads, gain_grads.transpose(0, 2, 1, 3)[None]
 

time: 117 us -> 108 us (0.923)
  the two profiles are of different devices: /device:TPU:1 before, /device:TPU:24 now
where the time goes in v3:
time: 108 us
  Pallas kernels  107 us (99%)
    pallas_call x1, Pallas kernels, per_device(): pl.pallas_call(kernel, out_shape=(jax.ShapeDtypeStruct((3, 4, TOKENS, HD)...  105 us

profile of v3, /device:TPU:24, one launch (start us, length us, event | category | flops | bytes accessed | tf_op | source)
XLA Modules:
  0.0 107.7 jit_solution(2538063793215016240)
XLA Ops:
  0.6 105.2 %sections_back.1 = (bf16[3,4,256,128]{3,2,1,0:T(8,128)(2,1)}, f32[2,12,2,128]{3,2,1,0:T(2,128)}) custom-call(bf16[3,4,256,128]{3,2,1,0:T(8,128)(2,1)} %bitcast.21, bf16[3,4,256,128]{3,2,1,0:T(8,128)(2,1)} %bitcast.22, f32[2,12,2,128]{3,2,1,0:T(2,128)} %bitcast.23), custom_call_target="tpu_custom_call" | custom-call | tf_op jit(solution)/shard_map/sections_back/pallas_call | solution.py:549
  105.8 1.9 %hand_over.1 = (bf16[3,4,256,128]{3,2,1,0:T(8,128)(2,1)}, f32[2,12,2,128]{3,2,1,0:T(2,128)}) custom-call(bf16[3,4,256,128]{3,2,1,0:T(8,128)(2,1)} %get-tuple-element.6.grads, f32[2,12,2,128]{3,2,1,0:T(2,128)} %get-tuple-element.7.gains), custom_call_target="tpu_custom_call" | custom-call | tf_op jit(solution)/shard_map/hand_over/pallas_call | solution.py:562

commit v4 on v3

--- a/solution.py
+++ b/solution.py
@@ -51,12 +51,12 @@
     return dxs, gq * SCALE, gk * SCALE
 
 
-def kernel(a_ref, og_ref, g_ref, out_ref, gout_ref,
+def kernel(a_ref, og_ref, g_ref, out_ref, gains_ref,
            l1a, a_s, og_s, gn, ys, yt, gt, dyt, dys, dxs, l1o,
            xf, xo, sp, spb, sq, sk, sn, sr, tx, tp, tpb, tq, tk, tn, trr,
-           gsum, gcol, gunit, gl1, ghop, gall,
+           gsum, gcol, gunit,
            s_a1, r_a1, s_a2, r_a2, s_og, r_og, s_gn, r_gn, s_y, r_y, s_g, r_g, s_dy, r_dy,
-           s_o1, r_o1, s_o2, r_o2, s_p1, r_p1, s_p2, r_p2, s_p3, r_p3, go):
+           s_o1, r_o1, s_o2, r_o2, s_p1, r_p1, s_p2, r_p2, go, go_first):
     seq = lax.axis_index("seq")
     x = lax.axis_index("pipe")
     dp_i = lax.axis_index("dp")
@@ -104,6 +104,9 @@
     def frame_device(i):
         return dev(x, (x + i + 4 - u_r) % 4 + 4 * ((c + 1) % 2), i, z_hi, u_c)
 
+    def first_frame(i):
+        return dev(0, (x + i + 4 - u_r) % 4 + 4 * ((c + 1) % 2), i, z_hi, u_c)
+
     def peers():
         for dx in (2, 1, 3, 0):
             for cc in (c, 1 - c) if dx else (1 - c,):
@@ -114,17 +117,11 @@
         xx = (x + j) % 4
         return xx, dev(xx, y, z_lo, z_hi, c)
 
-    def sample_units(m):
-        zl = (head_row(x) + m) % 4
-        for zh in range(2):
-            for cc in range(2):
-                yield dev(x, 4 * cc + (zl + 1 + m) % 4, zl, zh, (half + 1) % 2)
-
-    def sample_frames(i):
+    def sample_frames(s, i):
         y_f = (x + i + 4 - u_r) % 4 + 4 * ((c + 1) % 2)
         for zh in range(2):
             for cc in range(2):
-                yield dev(x, y_f, i, zh, cc)
+                yield dev(s, y_f, i, zh, cc)
 
     barrier = pltpu.get_barrier_semaphore()
 
@@ -134,33 +131,20 @@
     for _, to in peers():
         greet(to)
 
-    def is_me(to):
-        return (to["seq"] == seq) & (to["dp"] == dp_i)
-
-    own = active & ((x + z_lo + 4 - u_r) % 4 + 4 * ((c + 1) % 2) == y)
-
-    def greet_all(devices):
-        for to in devices:
-            @pl.when(jnp.logical_not(is_me(to)))
-            def _():
-                greet(to)
-
-    loop(0, 3, lambda m: greet_all(sample_units(m)))
+    loop(0, 3, lambda m: greet(unit_device(m)))
+    greet(dev(x, y, z_lo, 1 - z_hi, c))
+    greet(dev(x, y, z_lo, 1 - z_hi, 1 - c))
 
     @pl.when(active)
     def _():
-        loop(0, 4, lambda i: greet_all(sample_frames(i)))
-        @pl.when(own)
-        def _():
-            pl.semaphore_wait(barrier, 33)
-
-        @pl.when(jnp.logical_not(own))
-        def _():
-            pl.semaphore_wait(barrier, 35)
-
-    @pl.when(jnp.logical_not(active))
-    def _():
-        pl.semaphore_wait(barrier, 19)
+        loop(0, 4, lambda i: greet(frame_device(i)))
+
+    pl.semaphore_wait(barrier, 12 + 4 * active.astype(jnp.int32))
+
+    def is_me(to):
+        return (to["seq"] == seq) & (to["pipe"] == x) & (to["dp"] == dp_i)
+
+    own = (x + z_lo + 4 - u_r) % 4 + 4 * ((c + 1) % 2) == y
 
     def hop_a(m):
         copy(a_ref.at[m, head_row(x)], l1a.at[x, m], r_a1.at[x, m])
@@ -174,7 +158,9 @@
     def hops_a():
         loop(0, 3, lambda j: hop_a((j + z_lo) % 3))
 
-    hops_a()
+    @pl.when(jnp.logical_or(x == last, jnp.logical_not(active)))
+    def _():
+        hops_a()
 
     copy(g_ref, gn.at[x], r_gn)
     loop(1, 4, lambda j: send(g_ref, gn.at[x], s_gn, r_gn, along_x(j)[1]))
@@ -185,13 +171,18 @@
     loop(0, 3, send_og)
     gsum[...] = jnp.zeros_like(gsum)
 
-    def forward_a(s):
+    def forward_a(s, then=None):
         def one(j):
             m = (j + z_lo) % 3
             wait(l1a.at[s, m], r_a1.at[s, m])
             send(l1a.at[s, m], a_s.at[s, z_lo], s_a2.at[s], r_a2.at[s], unit_device(m))
 
-        loop(0, 3, one)
+        if then is None:
+            loop(0, 3, one)
+        else:
+            one(0)
+            then()
+            loop(1, 3, one)
 
     def hop_out(s, lo=0, hi=3):
         row = head_row(x)
@@ -212,19 +203,6 @@
 
             loop(lo, hi, one)
 
-    def hop_gains(s):
-        row = head_row(x)
-        wait(gl1.at[s], r_p2.at[s])
-        ghop[s] = jnp.sum(gl1[s], axis=1)
-
-        @pl.when(x == s)
-        def _():
-            copy(ghop.at[s], gall.at[row], r_p3)
-
-        @pl.when(x != s)
-        def _():
-            send(ghop.at[s], gall.at[row], s_p3.at[s], r_p3, dev(s, y, z_lo, z_hi, c))
-
     def share_gains(s):
         copy(gsum.at[s], gcol.at[s, d], r_p1.at[s])
         for _, to in peers():
@@ -235,17 +213,25 @@
         gunit[s] = jnp.sum(gcol[s], axis=0)
 
         def one(i):
-            at = gl1.at[s, u_m, z_hi * 2 + u_c]
-            for to in sample_frames(i):
+            at = gains_ref.at[u_r, u_m, z_hi * 2 + u_c]
+            for to in sample_frames(s, i):
                 @pl.when(is_me(to))
                 def _():
-                    copy(gunit.at[s], at, r_p2.at[s])
+                    copy(gunit.at[s], at, r_p2)
 
                 @pl.when(jnp.logical_not(is_me(to)))
                 def _():
-                    send(gunit.at[s], at, s_p2.at[s], r_p2.at[s], to)
+                    send(gunit.at[s], at, s_p2.at[s], r_p2, to)
 
         loop(0, 4, one)
+
+    def send_first(lo, hi):
+        loop(lo, hi, lambda i: send(
+            dxs.at[0, i], out_ref.at[u_m, u_r], s_o1.at[0], r_o2, first_frame(i)))
+
+    def ready_for_first():
+        loop(0, 3, lambda m: pl.semaphore_signal(
+            go_first, inc=1, device_id=unit_device(m), device_id_type=MESH))
 
     def send_out(s, lo, hi):
         loop(lo, hi, lambda i: send(
@@ -274,10 +260,10 @@
     def gain_row(s, l, j):
         return gn[s, l, u_h, j:j + 1, :]
 
-    def spatial_fwd(s):
+    def spatial_fwd(s, frames=range(4)):
         gq, gk = gain_row(s, 0, 0), gain_row(s, 0, 1)
         b = s % 2
-        for i in range(4):
+        for i in frames:
             ab = a_s[s, i]
             u = ab.astype(F32)
             (r,), (n,), (q,), (k,), (p,) = attend_fwd([u], gq, gk, None)
@@ -344,7 +330,12 @@
         part = slice(4 * first, 4 * first + 16)
         dyt[s, :, :, part, :] = xo.reshape(8, 4, 32, HD)[:, :, part, :].astype(BF)
 
-    forward_a(last)
+    def follow():
+        @pl.when(jnp.logical_and(x != last, active))
+        def _():
+            hops_a()
+
+    forward_a(last, follow)
 
     @pl.when(active)
     def _():
@@ -352,8 +343,10 @@
         to_tokens(og_s, gt.at[last], s_g.at[last], r_g.at[last])
         wait(gn, r_gn)
         wait(a_s.at[last], r_a2.at[last])
-        spatial_fwd(last)
-        to_tokens(ys.at[last], yt.at[last], s_y.at[last], r_y.at[last])
+        for part in range(2):
+            spatial_fwd(last, range(2 * part, 2 * part + 2))
+            to_tokens(ys.at[last], yt.at[last], s_y.at[last], r_y.at[last], 2 * part, 2)
+
         loop(0, 4, lambda i: pl.semaphore_signal(
             go, inc=1, device_id=frame_device(i), device_id_type=MESH))
         forward_a(last - 1)
@@ -388,18 +381,13 @@
 
             @pl.when(s == 0)
             def _():
-                hop_gains(3)
-                hop_gains(2)
+                ready_for_first()
 
             spatial_bwd(s, 0)
 
             @pl.when(s > 0)
             def _():
                 to_tokens(dxs.at[s], gt.at[before], s_g.at[before], r_g.at[before], 0, 2)
-
-            @pl.when(s == 0)
-            def _():
-                send_out(s, 0, 2)
 
             spatial_bwd(s, 2)
 
@@ -415,54 +403,29 @@
             def _():
                 send_out(s, 0, 4)
 
-            @pl.when(s == 0)
-            def _():
-                send_out(s, 2, 4)
-
         loop(0, SECTIONS, section)
         pl.semaphore_wait(go, 3)
+        hop_out(3)
+        pl.semaphore_wait(go_first, 4)
+        send_first(0, 4)
         unit_gains(0)
-        hop_gains(1)
-        hop_out(3)
         hop_out(2)
         hop_out(1)
 
     @pl.when(jnp.logical_not(active))
     def _():
+        ready_for_first()
         wait(gn, r_gn)
         pl.semaphore_wait(go, 3)
         loop(1, SECTIONS, lambda j: forward_a(last - j))
 
-        def relay(j):
-            hop_out(last - j)
-            hop_gains(last - j)
-
-        loop(0, SECTIONS - 1, relay)
-
-    hop_out(0)
-    hop_gains(0)
-
-    wait(gall, r_p3)
-    for row in range(4):
-        for m in range(3):
-            for l in range(2):
-                gout_ref[l, row + 4 * m] = gall[row, m, 2 * l:2 * l + 2]
-
-    wait(out_ref, r_o2)
+        loop(0, SECTIONS - 1, lambda j: hop_out(last - j))
 
     wait(l1a.at[pl.ds(0, 3)], s_a1)
     wait(og_s.at[pl.ds(0, 3)], s_og)
     wait(gn.at[pl.ds(0, 3)], s_gn)
 
-    def drain(s):
-        wait(l1a.at[s], s_a2.at[s])
-
-        @pl.when(x != s)
-        def _():
-            wait(l1o.at[s], s_o2.at[s])
-            wait(ghop.at[s], s_p3.at[s])
-
-    loop(0, SECTIONS, drain)
+    loop(0, SECTIONS, lambda s: wait(l1a.at[s], s_a2.at[s]))
 
     @pl.when(active)
     def _():
@@ -472,30 +435,57 @@
             wait(dyt.at[s, pl.ds(0, 7)], s_y.at[s])
             wait(dyt.at[s, pl.ds(0, 7)], s_g.at[s])
             wait(dyt.at[s, pl.ds(0, 7)], s_dy.at[s])
-            wait(dxs.at[s], s_o1.at[s])
+
+            @pl.when(s > 0)
+            def _():
+                wait(dxs.at[s], s_o1.at[s])
+
             wait(gcol.at[s, pl.ds(0, 7)], s_p1.at[s])
 
-            @pl.when(own)
+            @pl.when(own & (s == x))
             def _():
                 wait(slots.at[pl.ds(0, 15)], s_p2.at[s])
 
-            @pl.when(jnp.logical_not(own))
+            @pl.when(jnp.logical_not(own & (s == x)))
             def _():
                 wait(slots.at[pl.ds(0, 16)], s_p2.at[s])
 
         loop(0, SECTIONS, drain)
 
-
-def hand_over(grads, gains, grads_out, gains_out, buf, gbuf, s_in, s_out):
-    parts = [(grads.at[m], buf.at[m], grads_out.at[m]) for m in range(3)]
-    parts.append((gains, gbuf, gains_out))
-    first = [pltpu.make_async_copy(a, b, s_in.at[i]) for i, (a, b, _) in enumerate(parts)]
-    second = [pltpu.make_async_copy(b, c, s_out.at[i]) for i, (_, b, c) in enumerate(parts)]
+    wait(gains_ref, r_p2)
+    wait(out_ref, r_o2)
+
+    def drain(s):
+        @pl.when(x != s)
+        def _():
+            wait(l1o.at[s], s_o2.at[s])
+
+    loop(1, SECTIONS, drain)
+
+    @pl.when(active)
+    def _():
+        wait(dxs.at[0], s_o1.at[0])
+
+
+def hand_over(grads, gains, grads_out, gains_out, buf, gin, gbuf, s_in, s_out, s_g):
+    parts = [(m, row) for m in range(3) for row in range(4)]
+    first = [pltpu.make_async_copy(grads.at[p], buf.at[p], s_in.at[p]) for p in parts]
+    second = [pltpu.make_async_copy(buf.at[p], grads_out.at[p], s_out.at[p]) for p in parts]
+    arrive = pltpu.make_async_copy(gains, gin, s_g.at[0])
+    leave = pltpu.make_async_copy(gbuf, gains_out, s_g.at[1])
+    arrive.start()
     for one in first:
         one.start()
+    arrive.wait()
+    for m, row in parts:
+        total = jnp.sum(gin[row, m], axis=0)
+        for l in range(2):
+            gbuf[l, row + 4 * m] = total[2 * l:2 * l + 2]
+    leave.start()
     for one, other in zip(first, second):
         one.wait()
         other.start()
+    leave.wait()
     for one in second:
         one.wait()
 
@@ -538,22 +528,18 @@
         V((4, 4, HD), F32),
         V((4, 8, 4, HD), F32),
         V((4, 4, HD), F32),
-        V((4, 3, 4, 4, HD), F32),
-        V((4, 3, 4, HD), F32),
-        V((4, 3, 4, HD), F32),
         D, D(s43), D(s4), D(s4), D, D, D, D, D(s4), D(s4), D(s4), D(s4), D(s4), D(s4),
-        D(s4), D(s43), D(s4), D, D(s4), D(s4), D(s4), D(s4), D(s4), D, pltpu.SemaphoreType.REGULAR,
+        D(s4), D(s43), D(s4), D, D(s4), D(s4), D(s4), D, pltpu.SemaphoreType.REGULAR, pltpu.SemaphoreType.REGULAR,
     ]
-    vm = pl.BlockSpec(memory_space=pltpu.VMEM)
     hbm = pl.BlockSpec(memory_space=pl.ANY)
     grads, gain_grads = pl.pallas_call(
         kernel,
         out_shape=(
             jax.ShapeDtypeStruct((3, 4, TOKENS, HD), BF),
-            jax.ShapeDtypeStruct((2, HEADS, 2, HD), F32),
+            jax.ShapeDtypeStruct((4, 3, 4, 4, HD), F32),
         ),
         in_specs=[hbm, hbm, hbm],
-        out_specs=(hbm, vm),
+        out_specs=(hbm, hbm),
         scratch_shapes=scratch,
         compiler_params=pltpu.CompilerParams(
             has_side_effects=True, collective_id=0, vmem_limit_bytes=60 * 1024 * 1024),
@@ -563,11 +549,12 @@
         hand_over,
         out_shape=(
             jax.ShapeDtypeStruct(grads.shape, BF),
-            jax.ShapeDtypeStruct(gain_grads.shape, F32),
+            jax.ShapeDtypeStruct((2, HEADS, 2, HD), F32),
         ),
         in_specs=[hbm, hbm],
         out_specs=(hbm, hbm),
-        scratch_shapes=[V(grads.shape, BF), V(gain_grads.shape, F32), D(s4), D(s4)],
+        scratch_shapes=[V(grads.shape, BF), V(gain_grads.shape, F32),
+                        V((2, HEADS, 2, HD), F32), D((3, 4)), D((3, 4)), D((2,))],
         compiler_params=pltpu.CompilerParams(vmem_limit_bytes=60 * 1024 * 1024),
         name="hand_over",
     )(grads, gain_grads)

time: 108 us -> 105 us (0.972)
  the two profiles are of different devices: /device:TPU:24 before, /device:TPU:27 now
where the time goes in v4:
time: 105 us
  Pallas kernels  104 us (99%)
    pallas_call x1, Pallas kernels, per_device(): pl.pallas_call(kernel, out_shape=(jax.ShapeDtypeStruct((3, 4, TOKENS, HD)...  102 us
    pallas_call x1, Pallas kernels, per_device(): pl.pallas_call(hand_over, out_shape=(jax.ShapeDtypeStruct(grads.shape, BF...  2.34 us

profile of v4, /device:TPU:27, one launch (start us, length us, event | category | flops | bytes accessed | tf_op | source)
XLA Modules:
  0.0 105.0 jit_solution(6080387456393299379)
XLA Ops:
  0.6 102.0 %sections_back.1 = (bf16[3,4,256,128]{3,2,1,0:T(8,128)(2,1)}, f32[4,3,4,4,128]{4,3,2,1,0:T(4,128)}) custom-call(bf16[3,4,256,128]{3,2,1,0:T(8,128)(2,1)} %bitcast.21, bf16[3,4,256,128]{3,2,1,0:T(8,128)(2,1)} %bitcast.22, f32[2,12,2,128]{3,2,1,0:T(2,128)} %bitcast.23), custom_call_target="tpu_custom_call" | custom-call | tf_op jit(solution)/shard_map/sections_back/pallas_call | solution.py:535
  102.6 2.3 %hand_over.1 = (bf16[3,4,256,128]{3,2,1,0:T(8,128)(2,1)}, f32[2,12,2,128]{3,2,1,0:T(2,128)}) custom-call(bf16[3,4,256,128]{3,2,1,0:T(8,128)(2,1)} %get-tuple-element.6.grads, f32[4,3,4,4,128]{4,3,2,1,0:T(4,128)} %get-tuple-element.7.gains), custom_call_target="tpu_custom_call" | custom-call | tf_op jit(solution)/shard_map/hand_over/pallas_call | solution.py:548

commit v5 on v4

--- a/solution.py
+++ b/solution.py
@@ -146,17 +146,22 @@
 
     own = (x + z_lo + 4 - u_r) % 4 + 4 * ((c + 1) % 2) == y
 
-    def hop_a(m):
-        copy(a_ref.at[m, head_row(x)], l1a.at[x, m], r_a1.at[x, m])
-
-        def one(j):
-            xx, to = along_x(j)
-            send(a_ref.at[m, head_row(xx)], l1a.at[x, m], s_a1, r_a1.at[x, m], to)
-
-        loop(1, 4, one)
+    def piece(q):
+        m = (q // 2 + z_lo) % 3
+        return m, pl.ds(pl.multiple_of(q % 2 * 128, 128), 128), 2 * m + q % 2
 
     def hops_a():
-        loop(0, 3, lambda j: hop_a((j + z_lo) % 3))
+        def one(q):
+            m, rows, k = piece(q)
+            copy(a_ref.at[m, head_row(x), rows], l1a.at[x, m, rows], r_a1.at[x, k])
+
+            def to_plane(j):
+                xx, to = along_x(j)
+                send(a_ref.at[m, head_row(xx), rows], l1a.at[x, m, rows], s_a1, r_a1.at[x, k], to)
+
+            loop(1, 4, to_plane)
+
+        loop(0, 6, one)
 
     @pl.when(jnp.logical_or(x == last, jnp.logical_not(active)))
     def _():
@@ -172,17 +177,18 @@
     gsum[...] = jnp.zeros_like(gsum)
 
     def forward_a(s, then=None):
-        def one(j):
-            m = (j + z_lo) % 3
-            wait(l1a.at[s, m], r_a1.at[s, m])
-            send(l1a.at[s, m], a_s.at[s, z_lo], s_a2.at[s], r_a2.at[s], unit_device(m))
+        def one(q):
+            m, rows, k = piece(q)
+            wait(l1a.at[s, m, rows], r_a1.at[s, k])
+            send(l1a.at[s, m, rows], a_s.at[s, z_lo, rows], s_a2.at[s], r_a2.at[s],
+                 unit_device(m))
 
         if then is None:
-            loop(0, 3, one)
+            loop(0, 6, one)
         else:
-            one(0)
+            loop(0, 2, one)
             then()
-            loop(1, 3, one)
+            loop(2, 6, one)
 
     def hop_out(s, lo=0, hi=3):
         row = head_row(x)
@@ -251,11 +257,10 @@
 
     def to_frames(src, dst, ssem, rsem, first):
         mine = pl.ds(pl.multiple_of(d * 32 + first, 16), 16)
-        part = pl.ds(first, 16)
-        copy(src.at[d, :, part, :], dst.at[:, mine, :], rsem)
+        copy(src.at[d], dst.at[:, mine, :], rsem)
 
         for p, to in peers():
-            send(src.at[p, :, part, :], dst.at[:, mine, :], ssem, rsem, to)
+            send(src.at[p], dst.at[:, mine, :], ssem, rsem, to)
 
     def gain_row(s, l, j):
         return gn[s, l, u_h, j:j + 1, :]
@@ -325,10 +330,9 @@
              for b in four], gq, gk)
         for b, block in zip(four, dx):
             for t in range(4):
-                xo[pl.ds(b * 4 + t, FRAMES, stride=32), :] = block[t * 32:(t + 1) * 32]
+                xo[pl.ds((b - first) * 4 + t, FRAMES, stride=16), :] = block[t * 32:(t + 1) * 32]
         add_gains(s, 1, dgq, dgk)
-        part = slice(4 * first, 4 * first + 16)
-        dyt[s, :, :, part, :] = xo.reshape(8, 4, 32, HD)[:, :, part, :].astype(BF)
+        dyt[s, first // 4] = xo[...].astype(BF).reshape(8, 4, 16, HD)
 
     def follow():
         @pl.when(jnp.logical_and(x != last, active))
@@ -361,7 +365,7 @@
             by_token(gt.at[s])
             for part in range(2):
                 temporal_bwd(s, 4 * part)
-                to_frames(dyt.at[s], dys.at[s], s_dy.at[s], r_dy.at[s], 16 * part)
+                to_frames(dyt.at[s, part], dys.at[s], s_dy.at[s], r_dy.at[s, part], 16 * part)
 
             @pl.when(s > 1)
             def _():
@@ -377,12 +381,13 @@
             def _():
                 unit_gains(after)
 
-            wait(dys.at[s], r_dy.at[s])
+            wait(dys.at[s, pl.ds(0, 2)], r_dy.at[s, 0])
 
             @pl.when(s == 0)
             def _():
                 ready_for_first()
 
+            wait(dys.at[s, pl.ds(2, 2)], r_dy.at[s, 1])
             spatial_bwd(s, 0)
 
             @pl.when(s > 0)
@@ -406,11 +411,11 @@
         loop(0, SECTIONS, section)
         pl.semaphore_wait(go, 3)
         hop_out(3)
+        hop_out(1)
+        unit_gains(0)
         pl.semaphore_wait(go_first, 4)
         send_first(0, 4)
-        unit_gains(0)
         hop_out(2)
-        hop_out(1)
 
     @pl.when(jnp.logical_not(active))
     def _():
@@ -432,9 +437,9 @@
         slots = gcol.reshape(32, 4, HD)
 
         def drain(s):
-            wait(dyt.at[s, pl.ds(0, 7)], s_y.at[s])
-            wait(dyt.at[s, pl.ds(0, 7)], s_g.at[s])
-            wait(dyt.at[s, pl.ds(0, 7)], s_dy.at[s])
+            wait(yt.at[s, pl.ds(0, 7)], s_y.at[s])
+            wait(yt.at[s, pl.ds(0, 7)], s_g.at[s])
+            wait(yt.at[s, pl.ds(0, 7)], s_dy.at[s])
 
             @pl.when(s > 0)
             def _():
@@ -468,19 +473,19 @@
 
 
 def hand_over(grads, gains, grads_out, gains_out, buf, gin, gbuf, s_in, s_out, s_g):
-    parts = [(m, row) for m in range(3) for row in range(4)]
-    first = [pltpu.make_async_copy(grads.at[p], buf.at[p], s_in.at[p]) for p in parts]
-    second = [pltpu.make_async_copy(buf.at[p], grads_out.at[p], s_out.at[p]) for p in parts]
+    first = [pltpu.make_async_copy(grads.at[m], buf.at[m], s_in.at[m]) for m in range(3)]
+    second = [pltpu.make_async_copy(buf.at[m], grads_out.at[m], s_out.at[m]) for m in range(3)]
     arrive = pltpu.make_async_copy(gains, gin, s_g.at[0])
     leave = pltpu.make_async_copy(gbuf, gains_out, s_g.at[1])
     arrive.start()
     for one in first:
         one.start()
     arrive.wait()
-    for m, row in parts:
-        total = jnp.sum(gin[row, m], axis=0)
-        for l in range(2):
-            gbuf[l, row + 4 * m] = total[2 * l:2 * l + 2]
+    for row in range(4):
+        for m in range(3):
+            total = jnp.sum(gin[row, m], axis=0)
+            for l in range(2):
+                gbuf[l, row + 4 * m] = total[2 * l:2 * l + 2]
     leave.start()
     for one, other in zip(first, second):
         one.wait()
@@ -506,12 +511,12 @@
         V((4, 4, TOKENS, HD), BF),
         V((4, 8, 4, 32, HD), BF),
         V((4, 8, 4, 32, HD), BF),
-        V((4, 8, 4, 32, HD), BF),
+        V((4, 2, 8, 4, 16, HD), BF),
         V((4, 4, TOKENS, HD), BF),
         V((4, 4, TOKENS, HD), BF),
         V((4, 3, TOKENS, HD), BF),
         V((FRAMES * 32, HD), F32),
-        V((FRAMES * 32, HD), F32),
+        V((FRAMES * 16, HD), F32),
         V((2, 4, TOKENS, TOKENS), F32),
         V((2, 4, TOKENS, TOKENS), BF),
         V((2, 4, TOKENS, HD), BF),
@@ -528,7 +533,7 @@
         V((4, 4, HD), F32),
         V((4, 8, 4, HD), F32),
         V((4, 4, HD), F32),
-        D, D(s43), D(s4), D(s4), D, D, D, D, D(s4), D(s4), D(s4), D(s4), D(s4), D(s4),
+        D, D((SECTIONS, 6)), D(s4), D(s4), D, D, D, D, D(s4), D(s4), D(s4), D(s4), D(s4), D((SECTIONS, 2)),
         D(s4), D(s43), D(s4), D, D(s4), D(s4), D(s4), D, pltpu.SemaphoreType.REGULAR, pltpu.SemaphoreType.REGULAR,
     ]
     hbm = pl.BlockSpec(memory_space=pl.ANY)
@@ -554,7 +559,7 @@
         in_specs=[hbm, hbm],
         out_specs=(hbm, hbm),
         scratch_shapes=[V(grads.shape, BF), V(gain_grads.shape, F32),
-                        V((2, HEADS, 2, HD), F32), D((3, 4)), D((3, 4)), D((2,))],
+                        V((2, HEADS, 2, HD), F32), D((3,)), D((3,)), D((2,))],
         compiler_params=pltpu.CompilerParams(vmem_limit_bytes=60 * 1024 * 1024),
         name="hand_over",
     )(grads, gain_grads)

time: 105 us -> 104 us (level)
  the two profiles are of different devices: /device:TPU:27 before, /device:TPU:1 now
where the time goes in v5:
time: 104 us
  Pallas kernels  103 us (99%)
    pallas_call x1, Pallas kernels, per_device(): pl.pallas_call(kernel, out_shape=(jax.ShapeDtypeStruct((3, 4, TOKENS, HD)...  101 us

profile of v5, /device:TPU:1, one launch (start us, length us, event | category | flops | bytes accessed | tf_op | source)
XLA Modules:
  0.0 103.8 jit_solution(12308095342945629397)
XLA Ops:
  0.6 101.1 %sections_back.1 = (bf16[3,4,256,128]{3,2,1,0:T(8,128)(2,1)}, f32[4,3,4,4,128]{4,3,2,1,0:T(4,128)}) custom-call(bf16[3,4,256,128]{3,2,1,0:T(8,128)(2,1)} %bitcast.21, bf16[3,4,256,128]{3,2,1,0:T(8,128)(2,1)} %bitcast.22, f32[2,12,2,128]{3,2,1,0:T(2,128)} %bitcast.23), custom_call_target="tpu_custom_call" | custom-call | tf_op jit(solution)/shard_map/sections_back/pallas_call | solution.py:540
  101.7 2.0 %hand_over.1 = (bf16[3,4,256,128]{3,2,1,0:T(8,128)(2,1)}, f32[2,12,2,128]{3,2,1,0:T(2,128)}) custom-call(bf16[3,4,256,128]{3,2,1,0:T(8,128)(2,1)} %get-tuple-element.6.grads, f32[4,3,4,4,128]{4,3,2,1,0:T(4,128)} %get-tuple-element.7.gains), custom_call_target="tpu_custom_call" | custom-call | tf_op jit(solution)/shard_map/hand_over/pallas_call | solution.py:553

commit v6 on v5

--- a/solution.py
+++ b/solution.py
@@ -235,6 +235,10 @@
         loop(lo, hi, lambda i: send(
             dxs.at[0, i], out_ref.at[u_m, u_r], s_o1.at[0], r_o2, first_frame(i)))
 
+    def next_frames(s):
+        loop(0, 4, lambda i: pl.semaphore_signal(
+            go.at[s], inc=1, device_id=frame_device(i), device_id_type=MESH))
+
     def ready_for_first():
         loop(0, 3, lambda m: pl.semaphore_signal(
             go_first, inc=1, device_id=unit_device(m), device_id_type=MESH))
@@ -351,8 +355,7 @@
             spatial_fwd(last, range(2 * part, 2 * part + 2))
             to_tokens(ys.at[last], yt.at[last], s_y.at[last], r_y.at[last], 2 * part, 2)
 
-        loop(0, 4, lambda i: pl.semaphore_signal(
-            go, inc=1, device_id=frame_device(i), device_id_type=MESH))
+        next_frames(last - 1)
         forward_a(last - 1)
         wait(yt.at[last], r_y.at[last])
         temporal_fwd(last)
@@ -369,6 +372,7 @@
 
             @pl.when(s > 1)
             def _():
+                next_frames(jnp.maximum(s - 2, 0))
                 forward_a(jnp.maximum(s - 2, 0))
 
             @pl.when(s > 0)
@@ -409,7 +413,7 @@
                 send_out(s, 0, 4)
 
         loop(0, SECTIONS, section)
-        pl.semaphore_wait(go, 3)
+        loop(0, last, lambda s: pl.semaphore_wait(go.at[s], 3))
         hop_out(3)
         hop_out(1)
         unit_gains(0)
@@ -421,8 +425,12 @@
     def _():
         ready_for_first()
         wait(gn, r_gn)
-        pl.semaphore_wait(go, 3)
-        loop(1, SECTIONS, lambda j: forward_a(last - j))
+
+        def next_section(j):
+            pl.semaphore_wait(go.at[last - j], 3)
+            forward_a(last - j)
+
+        loop(1, SECTIONS, next_section)
 
         loop(0, SECTIONS - 1, lambda j: hop_out(last - j))
 
@@ -534,7 +542,7 @@
         V((4, 8, 4, HD), F32),
         V((4, 4, HD), F32),
         D, D((SECTIONS, 6)), D(s4), D(s4), D, D, D, D, D(s4), D(s4), D(s4), D(s4), D(s4), D((SECTIONS, 2)),
-        D(s4), D(s43), D(s4), D, D(s4), D(s4), D(s4), D, pltpu.SemaphoreType.REGULAR, pltpu.SemaphoreType.REGULAR,
+        D(s4), D(s43), D(s4), D, D(s4), D(s4), D(s4), D, pltpu.SemaphoreType.REGULAR((3,)), pltpu.SemaphoreType.REGULAR,
     ]
     hbm = pl.BlockSpec(memory_space=pl.ANY)
     grads, gain_grads = pl.pallas_call(

time: 104 us -> 106 us (1.019)
  the two profiles are of different devices: /device:TPU:1 before, /device:TPU:17 now
where the time goes in v6:
time: 106 us; the launch traced here: 105 us
  Pallas kernels  105 us (99%)
    pallas_call x1, Pallas kernels, per_device(): pl.pallas_call(kernel, out_shape=(jax.ShapeDtypeStruct((3, 4, TOKENS, HD)...  103 us

profile of v6, /device:TPU:17, one launch (start us, length us, event | category | flops | bytes accessed | tf_op | source)
XLA Modules:
  0.0 105.4 jit_solution(13765160477951395978)
XLA Ops:
  0.6 102.7 %sections_back.1 = (bf16[3,4,256,128]{3,2,1,0:T(8,128)(2,1)}, f32[4,3,4,4,128]{4,3,2,1,0:T(4,128)}) custom-call(bf16[3,4,256,128]{3,2,1,0:T(8,128)(2,1)} %bitcast.21, bf16[3,4,256,128]{3,2,1,0:T(8,128)(2,1)} %bitcast.22, f32[2,12,2,128]{3,2,1,0:T(2,128)} %bitcast.23), custom_call_target="tpu_custom_call" | custom-call | tf_op jit(solution)/shard_map/sections_back/pallas_call | solution.py:548
  103.4 2.0 %hand_over.1 = (bf16[3,4,256,128]{3,2,1,0:T(8,128)(2,1)}, f32[2,12,2,128]{3,2,1,0:T(2,128)}) custom-call(bf16[3,4,256,128]{3,2,1,0:T(8,128)(2,1)} %get-tuple-element.6.grads, f32[4,3,4,4,128]{4,3,2,1,0:T(4,128)} %get-tuple-element.7.gains), custom_call_target="tpu_custom_call" | custom-call | tf_op jit(solution)/shard_map/hand_over/pallas_call | solution.py:561
